TPU v7x, 128 devices: a whole 4x4x4 slice. The times are simulated.
128 devices in a mesh: gx: 16 (over z_lo, y, core), gy: 8 (over x, z_hi).
Axes of the slice: x: 4, y: 4, z: 4 (z_hi: 2, z_lo: 2; z = z_hi * 2 + z_lo), core: 2. Of those that a mesh axis runs over, the one named last changes fastest.
Arguments:
- probability: float32 [16, 16, 64, 2048], P('gx', None, None, 'gy'), may hold values from 0 to 1
- extent: int32 [4], replicated, may hold values from 4 to 1019, as said below
- slab_width: int32 [4], replicated, may hold values from 1 to 4, as said below
- rate_const: float32 [8], replicated, may hold values from 0.25 to 1.5
- hill_const: float32 [8], replicated, may hold values from 0.1 to 1
- stoichiometry: int32 [8, 4], replicated, may hold values from -1 to 1, as said below
- new_owner: int32 [16, 8, 1024, 1], P('gx', 'gy'), may hold values from 0 to 127; in each aligned block of 1024 rows (0 to 1023, 1024 to 2047, ..., all dimensions but the last counted through in order) at most 16 rows name the same one
Outputs:
- moved_bricks: float32 [128, 128, 16, 256], P(('gx', 'gy'))
Inputs may be any that keep to these rules, and one draw needn't show every extreme that they name: `stoichiometry`: every row has one nonzero entry, +1 or -1; every species is raised by exactly one reaction and lowered by exactly one. extent[d] lies from 12 below to 5 below the lattice's cells along species d (16, 1024, 64, 32). `slab_width`: at least one entry equals 4. `new_owner`: among the 1024 bricks of one device, at most 16 have the same new owner.
All inputs are finite; a program needn't handle non-finite values.
Results may differ from a plain program's by a relative error of at most 0.000073.
Values sent between devices are 32-bit elements; how exact they have to be, the bound alone decides.
A program may use at most 128 MiB of HBM per device.

v0:
```python
import functools

import jax
import jax.numpy as jnp
from jax import lax
from jax.experimental import pallas as pl
from jax.experimental.pallas import tpu as pltpu
from jax.sharding import PartitionSpec as P

MESH = pl.DeviceIdType.MESH
F32 = jnp.float32
BF16 = jnp.bfloat16

time_step = 0.15
GX, GY, DEVICES = 16, 8, 128
LATTICE = (16, 1024, 64, 32)
N0, ROWS, PLANES, N4 = 16, 64, 8, 32
LANES = 128
SLOTS = 16
OLD0 = 11
PAD = 8
ALL = ROWS + 2 * PAD
FIRST = 4
GROUPS = 9
BLOCK = 512


def advance(
    params, owner, prob, row_low, row_high, plane_low, plane_high, corner_low, corner_high, sent,
    u0, u1, u2, u3, xb, onehot, prefix, ones,
    t_r0, t_f1, t_r1, t_d, t_r2, t_f2, t_f3, t_n, t_mask, target,
):
    gx = lax.axis_index("gx")
    gy = lax.axis_index("gy")

    extent = [params[d] for d in range(4)]
    edge = [params[d] + params[4 + d] for d in range(4)]

    def pick(start, species, sign):
        total = jnp.float32(0.0)
        for r in range(8):
            total = total + jnp.where(params[24 + 8 * species + r] == sign, params[start + r], jnp.float32(0.0))
        return total

    rise_rate = [pick(8, d, 1.0) for d in range(4)]
    rise_hill = [pick(16, d, 1.0) for d in range(4)]
    fall_rate = [pick(8, d, -1.0) for d in range(4)]

    def rise(d, x):
        scaled = x / jnp.full(x.shape, rise_hill[d])
        return jnp.full(x.shape, rise_rate[d]) / (1.0 + scaled * scaled)

    def fall(d, x):
        return (2.0 * fall_rate[d]) * x

    def frac(n, d):
        return n.astype(F32) * (1.0 / LATTICE[d])

    steps = [time_step / j for j in (4.0, 3.0, 2.0, 1.0)]

    n1 = (gx * ROWS - PAD + LATTICE[1] + lax.broadcasted_iota(jnp.int32, (ALL, LANES), 0)) & (LATTICE[1] - 1)
    rise_0 = rise(0, frac(n1, 1))
    leave_1 = rise_0 + fall(1, frac(n1, 1))
    fall_1 = fall(1, frac((n1 + 1) & (LATTICE[1] - 1), 1))
    in_1 = jnp.where(n1.astype(F32) < edge[1], 1.0, 0.0)
    for q in range(4):
        t_r0[q] = steps[q] * rise_0
        t_f1[q] = steps[q] * fall_1
    lane8 = lax.broadcasted_iota(jnp.int32, (8, LANES), 1)
    n3 = lane8 & (N4 - 1)
    rise_2 = rise(2, frac(n3, 3))
    leave_3 = rise_2 + fall(3, frac(n3, 3))
    fall_3 = fall(3, frac((n3 + 1) & (N4 - 1), 3))
    in_3 = jnp.where(n3.astype(F32) < edge[3], 1.0, 0.0)
    for q in range(4):
        t_f3[q] = steps[q] * fall_3
    for t in range(4):
        n2 = (gy * PLANES + 4 * (t - 1) + LATTICE[2] + (lane8 >> 5)) & (LATTICE[2] - 1)
        rise_1 = rise(1, frac(n2, 2))
        leave_23 = leave_3 + rise_1 + fall(2, frac(n2, 2))
        fall_2 = fall(2, frac((n2 + 1) & (LATTICE[2] - 1), 2))
        in_2 = jnp.where(n2.astype(F32) < edge[2], 1.0, 0.0)
        old_23 = (n2.astype(F32) < extent[2]) & (n3.astype(F32) < extent[3])
        old_1 = n1.astype(F32) < extent[1]
        t_mask[t] = jnp.where(
            old_1 & jnp.concatenate([old_23] * (ALL // 8), axis=0), extent[0], 0.0
        )
        rise_1 = jnp.concatenate([rise_1] * (ALL // 8), axis=0)
        leave_23 = jnp.concatenate([leave_23] * (ALL // 8), axis=0)
        for q in range(4):
            t_r2[q, t] = steps[q] * (rise_2 * in_2)
            t_f2[q, t] = steps[q] * fall_2
            t_r1[q, t] = steps[q] * (rise_1 * in_1)
            t_d[q, t] = (-steps[q]) * (leave_1 + leave_23)

    def species_zero(n0, _):
        here = jnp.full((8, LANES), n0, jnp.int32)
        rise_3 = rise(3, frac(here, 0))
        leave_0 = rise_3 + fall(0, frac(here, 0))
        fall_0 = fall(0, frac(here + 1, 0))
        in_0 = jnp.where(here.astype(F32) < edge[0], 1.0, 0.0)
        for q in range(4):
            t_n[q, n0, 0] = steps[q] * (rise_3 * in_3)
            t_n[q, n0, 1] = steps[q] * fall_0
            t_n[q, n0, 2] = (-steps[q]) * leave_0
            t_n[q, n0, 3] = in_0
        return 0

    lax.fori_loop(0, N0 - 1, species_zero, 0)

    zero = jnp.zeros((ALL, LANES), F32)
    for t in range(4):
        for u, ks in (
            (u0, (0, 12, 13, 14, 15, 16)), (u1, (0, 13, 14)), (u2, (0, 14, 15)), (u3, (0, 15, 16))
        ):
            for k in ks:
                u[t, k] = zero
    xb[pl.ds((N0 - 1) * ROWS, ROWS), :] = jnp.zeros((ROWS, 4 * LANES), BF16)

    prefix[...] = jnp.where(
        lax.broadcasted_iota(jnp.int32, (128, 128), 0) < lax.broadcasted_iota(jnp.int32, (128, 128), 1), 1.0, 0.0
    ).astype(BF16)
    ones[...] = jnp.ones((128, 128), BF16)
    running = jnp.zeros((DEVICES, 128), F32)
    peer = lax.broadcasted_iota(jnp.int32, (DEVICES, 128), 0)
    for b in range(8):
        part = owner[:, pl.ds(b * 128, 128)]
        hit = jnp.where(peer == part, 1.0, 0.0)
        hit16 = hit.astype(BF16)
        count = running + jnp.dot(hit16, prefix[...], preferred_element_type=F32)
        running = running + jnp.dot(hit16, ones[...], preferred_element_type=F32)
        rank = jnp.sum(hit * count, axis=0, keepdims=True)
        target[:, pl.ds(b * 128, 128)] = part.astype(F32) * float(SLOTS) + rank

    def one_hot(i, _):
        row = lax.broadcasted_iota(jnp.int32, (32, 1024), 0) + i * 32
        onehot[pl.ds(pl.multiple_of(i * 32, 32), 32), :] = jnp.where(
            row.astype(F32) == target[...], 1.0, 0.0
        ).astype(BF16)
        return 0

    lax.fori_loop(0, DEVICES * SLOTS // 32, one_hot, 0)

    def prepare(n0, _):
        def put(t, row, count, values):
            rows = pl.ds(row, count)
            u0[t, n0 + 1, rows, :] = jnp.where(n0.astype(F32) < t_mask[t, rows, :], values, 0.0)

        for h in range(2):
            lanes = pl.ds(h * LANES, LANES)
            put(1 + h, 0, PAD, row_low[n0, :, lanes])
            put(1 + h, PAD + ROWS, PAD, row_high[n0, :, lanes])
            put(1 + h, PAD, ROWS, prob[n0, :, lanes])
        for t, plane, corner in ((0, plane_low, corner_low), (3, plane_high, corner_high)):
            put(t, PAD, ROWS, plane[n0])
            put(t, 0, PAD, corner[n0])
            put(t, PAD + ROWS, 4, corner[n0, pl.ds(0, 4), :])
        return 0

    lax.fori_loop(0, OLD0, prepare, 0)

    lane = lax.broadcasted_iota(jnp.int32, (8, LANES), 1)
    first_plane = lane < N4
    last_plane = lane >= LANES - N4

    def stage(q, src, dst):
        last = q == 3

        def body(n0, _):
            r3, f0, l0, m0 = (t_n[q, n0, i] for i in range(4))
            kept = {1: [], 2: []}
            for g in range(8 if last else GROUPS):
                row = 8 * g + (PAD if last else FIRST)
                rows = pl.ds(row, 8)
                r0 = t_r0[q, rows, :] * m0
                f1 = t_f1[q, rows, :]
                centre = [src[a, n0 + 1, rows, :] for a in range(4)]
                up = [pltpu.roll(c, N4, 1) for c in centre]
                down = [pltpu.roll(c, LANES - N4, 1) for c in centre]
                for a in ((1, 2) if last else range(4)):
                    c = centre[a]
                    from_below = jnp.where(first_plane, up[a - 1], up[a]) if a > 0 else up[a]
                    from_above = jnp.where(last_plane, down[a + 1], down[a]) if a < 3 else down[a]
                    acc = u0[a, n0 + 1, rows, :] + (t_d[q, a, rows, :] + l0) * c
                    acc = acc + (r0 * src[a, n0, rows, :] + f0 * src[a, n0 + 2, rows, :])
                    acc = acc + (
                        t_r1[q, a, rows, :] * src[a, n0 + 1, pl.ds(row - 1, 8), :]
                        + f1 * src[a, n0 + 1, pl.ds(row + 1, 8), :]
                    )
                    acc = acc + (t_r2[q, a] * from_below + t_f2[q, a] * from_above)
                    acc = acc + (r3 * pltpu.roll(c, 1, 1) + t_f3[q] * pltpu.roll(c, LANES - 1, 1))
                    if last:
                        kept[a].append(acc)
                    else:
                        dst[a, n0 + 1, rows, :] = acc
                if last and g % 2 == 1:
                    place = pl.ds(pl.multiple_of(n0 * ROWS + 8 * (g - 1), 16), 16)
                    for a in (1, 2):
                        pair = jnp.concatenate(kept[a], axis=0)
                        kept[a] = []
                        high = pair.astype(BF16)
                        low = (pair - high.astype(F32)).astype(BF16)
                        dst[place, pl.ds((a - 1) * LANES, LANES)] = high
                        dst[place, pl.ds((a + 1) * LANES, LANES)] = low
            return 0

        lax.fori_loop(0, 12 + q, body, 0)

    stage(0, u0, u1)
    stage(1, u1, u2)
    stage(2, u2, u3)
    stage(3, u3, xb)

    def permute(i, _):
        place = pl.ds(pl.multiple_of(i * BLOCK, BLOCK), BLOCK)
        both = jnp.dot(onehot[place, :], xb[...], preferred_element_type=F32)
        sent[place, :] = both[:, :2 * LANES] + both[:, 2 * LANES:]
        return 0

    lax.fori_loop(0, DEVICES * SLOTS // BLOCK, permute, 0)


def ring(values, axis, shift):
    count = lax.axis_size(axis)
    return lax.ppermute(values, axis, [(i, (i + shift) % count) for i in range(count)])


def shards(probability, extent, slab_width, rate_const, hill_const, stoichiometry, new_owner):
    vmem = pltpu.VMEM
    field = probability[0]
    inner = field[:OLD0]
    row_low = ring(inner[:, ROWS - PAD:], "gx", 1)
    row_high = ring(inner[:, :PAD], "gx", -1)
    plane_low = ring(inner[:, :, LANES:], "gy", 1)
    plane_high = ring(inner[:, :, :LANES], "gy", -1)
    corner = jnp.concatenate([row_high[:, :4], row_low[:, 4:]], axis=1)
    corner_low = ring(corner[:, :, LANES:], "gy", 1)
    corner_high = ring(corner[:, :, :LANES], "gy", -1)
    params = jnp.concatenate(
        [extent.astype(F32), slab_width.astype(F32), rate_const, hill_const, stoichiometry.T.reshape(32).astype(F32)]
    )
    whole = pl.BlockSpec(memory_space=pltpu.VMEM)
    sent = pl.pallas_call(
        advance,
        out_shape=jax.ShapeDtypeStruct((DEVICES * SLOTS, PLANES * N4), F32),
        in_specs=[pl.BlockSpec(memory_space=pltpu.SMEM)] + [whole] * 8,
        out_specs=whole,
        scratch_shapes=[
            vmem((4, N0 + 1, ALL, LANES), F32),
            vmem((4, N0 + 1, ALL, LANES), F32),
            vmem((4, N0 + 1, ALL, LANES), F32),
            vmem((4, N0 + 1, ALL, LANES), F32),
            vmem((N0 * ROWS, 4 * LANES), BF16),
            vmem((DEVICES * SLOTS, N0 * ROWS), BF16),
            vmem((128, 128), BF16),
            vmem((128, 128), BF16),
            vmem((4, ALL, LANES), F32),
            vmem((4, ALL, LANES), F32),
            vmem((4, 4, ALL, LANES), F32),
            vmem((4, 4, ALL, LANES), F32),
            vmem((4, 4, 8, LANES), F32),
            vmem((4, 4, 8, LANES), F32),
            vmem((4, 8, LANES), F32),
            vmem((4, N0, 4, 8, LANES), F32),
            vmem((4, ALL, LANES), F32),
            vmem((1, N0 * ROWS), F32),
        ],
        compiler_params=pltpu.CompilerParams(vmem_limit_bytes=40 * 1024 * 1024),
        name="advance",
    )(
        params, new_owner.reshape(1, N0 * ROWS), field, row_low, row_high, plane_low, plane_high,
        corner_low, corner_high,
    )
    moved = lax.all_to_all(
        sent.reshape(DEVICES, SLOTS, PLANES * N4), ("gx", "gy"), split_axis=0, concat_axis=0, tiled=True
    )
    return moved[None]


def solution(mesh):
    in_specs = (P("gx", None, None, "gy"), P(), P(), P(), P(), P(), P("gx", "gy", None, None))
    out_specs = P(("gx", "gy"), None, None, None)
    return jax.shard_map(shards, mesh=mesh, in_specs=in_specs, out_specs=out_specs, check_vma=False)
```

profile of v0, /device:TPU:0, one launch (start us, length us, event | category | flops | bytes accessed | tf_op | source)
XLA Modules:
  0.0 83.8 jit_solution(9799202832464019194)
XLA Ops:
  0.0 0.0 copy-start.3
  0.0 0.0 copy-start.1
  0.0 1.3 %slice_bitcast_fusion = f32[11,64,256]{2,1,0:T(8,128)S(1)} fusion(f32[1,16,64,256]{3,2,1,0:T(8,128)} %param.7), kind=kLoop, calls=%fused_computation | loop fusion | bytes 1441792 | tf_op jit(solution)/shard_map/slice | solution.py:231
  1.3 4.0 %collective-permute-start.1 = (f32[11,8,256]{2,1,0:T(8,128)S(1)}, f32[11,8,256]{2,1,0:T(8,128)S(1)}, u32[]{:S(2)}, u32[]{:S(2)}) collective-permute-start(f32[11,8,256]{2,1,0:T(8,128)S(1)} %get-tuple-element.7), channel_id=1, source_target_pairs={{0,120},{8,0},{16,8},{24,16},{32,24},{40,32},{48,40},{56,48},{64,5... | collective-permute-start | bytes 270344 | tf_op jit(solution)/shard_map/ppermute | solution.py:225
  5.3 0.0 collective-permute-start
  5.3 0.1 fusion.1
  5.4 5.8 %collective-permute-start.3 = (f32[11,64,128]{2,1,0:T(8,128)S(1)}, f32[11,64,128]{2,1,0:T(8,128)S(1)}, u32[]{:S(2)}, u32[]{:S(2)}) collective-permute-start(f32[11,64,128]{2,1,0:T(8,128)S(1)} %get-tuple-element.5), channel_id=1, source_target_pairs={{0,7},{1,0},{2,1},{3,2},{4,3},{5,4},{6,5},{7,6},{8,15},{9,8},{10,9... | collective-permute-start | bytes 1081352 | tf_op jit(solution)/shard_map/ppermute | solution.py:225
  11.2 0.0 collective-permute-start.2
  11.2 0.0 collective-permute-done.1.row_high
  11.2 1.2 %collective-permute-done.row_low = f32[11,8,256]{2,1,0:T(8,128)S(1)} collective-permute-done((f32[11,8,256]{2,1,0:T(8,128)S(1)}, f32[11,8,256]{2,1,0:T(8,128)S(1)}, u32[]{:S(2)}, u32[]{:S(2)}) %collective-permute-start) | collective-permute-done | bytes 90144 | tf_op jit(solution)/shard_map/ppermute | solution.py:225
  12.5 5.8 %collective-permute-start.5 = (f32[11,8,128]{2,1,0:T(8,128)S(1)}, f32[11,8,128]{2,1,0:T(8,128)S(1)}, u32[]{:S(2)}, u32[]{:S(2)}) collective-permute-start(f32[11,8,128]{2,1,0:T(8,128)S(1)} %get-tuple-element.9), channel_id=1, source_target_pairs={{0,7},{1,0},{2,1},{3,2},{4,3},{5,4},{6,5},{7,6},{8,15},{9,8},{10,9... | collective-permute-start | bytes 135176 | tf_op jit(solution)/shard_map/ppermute | solution.py:225
  18.3 0.0 collective-permute-start.4
  18.3 0.0 copy-done.2
  18.3 0.1 convert_element_type.19
  18.4 0.0 copy-done.4
  18.4 0.1 concatenate.6.params
  18.5 8.0 %collective-permute-done.5.corner_high = f32[11,8,128]{2,1,0:T(8,128)S(1)} collective-permute-done((f32[11,8,128]{2,1,0:T(8,128)S(1)}, f32[11,8,128]{2,1,0:T(8,128)S(1)}, u32[]{:S(2)}, u32[]{:S(2)}) %collective-permute-start.5) | collective-permute-done | bytes 45088 | tf_op jit(solution)/shard_map/ppermute | solution.py:225
  26.5 0.0 collective-permute-done.4.corner_low
  26.5 0.0 collective-permute-done.3.plane_high
  26.5 0.0 collective-permute-done.2.plane_low
  26.5 0.0 copy-done
  26.5 17.3 %advance.1 = f32[2048,256]{1,0:T(8,128)S(1)} custom-call(f32[56]{0:T(128)S(1)} %concatenate.6.params, s32[1,1024]{1,0:T(1,128)S(1)} %bitcast.10, f32[16,64,256]{2,1,0:T(8,128)S(1)} %bitcast.9, f32[11,8,256]{2,1,0:T(8,128)S(1)} %collective-permute-done.row_low, f32[11,8,256]{2,1,0:T(8,128)S(1)} %collective-permute-done.1.row_high, ...), custom_call_target="tpu_custom_call" | custom-call | tf_op jit(solution)/shard_map/advance/pallas_call | solution.py:243
  43.9 38.6 %all_to_all.5 = f32[128,16,256]{2,1,0:T(8,128)S(1)} all-to-all(f32[128,16,256]{2,1,0:T(8,128)S(1)} %bitcast.8), channel_id=1, replica_groups=mesh['gx'=16,'gy'=8] {'gx','gy'}, dimensions={0} | all-to-all | bytes 4194304 | tf_op jit(solution)/shard_map/all_to_all | solution.py:274
  82.4 1.3 %copy.9 = f32[1,128,16,256]{3,2,1,0:T(8,128)} copy(f32[1,128,16,256]{3,2,1,0:T(8,128)S(1)} %bitcast.11) | data formatting | bytes 4194304
  (16 shorter events, 0.1 us)
Async XLA Ops:
  0.0 26.5 %copy-start = (f32[1,16,64,256]{3,2,1,0:T(8,128)S(1)}, f32[1,16,64,256]{3,2,1,0:T(8,128)}, u32[]{:S(2)}) copy-start(f32[1,16,64,256]{3,2,1,0:T(8,128)} %param.7) | copy-start | bytes 3145732
  0.0 18.3 %copy-start.2 = (s32[8,4]{0,1:T(4,128)S(1)}, s32[8,4]{0,1:T(4,128)}, u32[]{:S(2)}) copy-start(s32[8,4]{0,1:T(4,128)} %param.12) | copy-start | bytes 388
  0.0 18.3 %copy-start.5 = (s32[4]{0:T(128)S(1)}, s32[4]{0:T(128)}, u32[]{:S(2)}) copy-start(s32[4]{0:T(128)} %param.8) | copy-start | bytes 52
  0.0 18.3 %copy-start.6 = (s32[4]{0:T(128)S(1)}, s32[4]{0:T(128)}, u32[]{:S(2)}) copy-start(s32[4]{0:T(128)} %param.9) | copy-start | bytes 52
  0.0 18.4 %copy-start.4 = (f32[8]{0:T(128)S(1)}, f32[8]{0:T(128)}, u32[]{:S(2)}) copy-start(f32[8]{0:T(128)} %param.11) | copy-start | bytes 100
  0.0 18.4 %copy-start.3 = (f32[8]{0:T(128)S(1)}, f32[8]{0:T(128)}, u32[]{:S(2)}) copy-start(f32[8]{0:T(128)} %param.10) | copy-start | bytes 100
  0.0 26.5 %copy-start.1 = (s32[1,1,1024,1]{2,3,1,0:T(1,128)S(1)}, s32[1,1,1024,1]{2,3,1,0:T(1,128)}, u32[]{:S(2)}) copy-start(s32[1,1,1024,1]{2,3,1,0:T(1,128)} %param.13) | copy-start | bytes 12292
  1.3 9.9 %collective-permute-start.1 = (f32[11,8,256]{2,1,0:T(8,128)S(1)}, f32[11,8,256]{2,1,0:T(8,128)S(1)}, u32[]{:S(2)}, u32[]{:S(2)}) collective-permute-start(f32[11,8,256]{2,1,0:T(8,128)S(1)} %get-tuple-element.7), channel_id=1, source_target_pairs={{0,120},{8,0},{16,8},{24,16},{32,24},{40,32},{48,40},{56,48},{64,5... | collective-permute-start | bytes 270344 | tf_op jit(solution)/shard_map/ppermute | solution.py:225
  5.3 7.1 %collective-permute-start = (f32[11,8,256]{2,1,0:T(8,128)S(1)}, f32[11,8,256]{2,1,0:T(8,128)S(1)}, u32[]{:S(2)}, u32[]{:S(2)}) collective-permute-start(f32[11,8,256]{2,1,0:T(8,128)S(1)} %get-tuple-element.8), channel_id=1, source_target_pairs={{0,8},{8,16},{16,24},{24,32},{32,40},{40,48},{48,56},{56,64},{64,7... | collective-permute-start | bytes 270344 | tf_op jit(solution)/shard_map/ppermute | solution.py:225
  5.4 21.1 %collective-permute-start.3 = (f32[11,64,128]{2,1,0:T(8,128)S(1)}, f32[11,64,128]{2,1,0:T(8,128)S(1)}, u32[]{:S(2)}, u32[]{:S(2)}) collective-permute-start(f32[11,64,128]{2,1,0:T(8,128)S(1)} %get-tuple-element.5), channel_id=1, source_target_pairs={{0,7},{1,0},{2,1},{3,2},{4,3},{5,4},{6,5},{7,6},{8,15},{9,8},{10,9... | collective-permute-start | bytes 1081352 | tf_op jit(solution)/shard_map/ppermute | solution.py:225
  11.2 15.3 %collective-permute-start.2 = (f32[11,64,128]{2,1,0:T(8,128)S(1)}, f32[11,64,128]{2,1,0:T(8,128)S(1)}, u32[]{:S(2)}, u32[]{:S(2)}) collective-permute-start(f32[11,64,128]{2,1,0:T(8,128)S(1)} %get-tuple-element.6), channel_id=1, source_target_pairs={{0,1},{1,2},{2,3},{3,4},{4,5},{5,6},{6,7},{7,0},{8,9},{9,10},{10,1... | collective-permute-start | bytes 1081352 | tf_op jit(solution)/shard_map/ppermute | solution.py:225
  12.5 14.0 %collective-permute-start.5 = (f32[11,8,128]{2,1,0:T(8,128)S(1)}, f32[11,8,128]{2,1,0:T(8,128)S(1)}, u32[]{:S(2)}, u32[]{:S(2)}) collective-permute-start(f32[11,8,128]{2,1,0:T(8,128)S(1)} %get-tuple-element.9), channel_id=1, source_target_pairs={{0,7},{1,0},{2,1},{3,2},{4,3},{5,4},{6,5},{7,6},{8,15},{9,8},{10,9... | collective-permute-start | bytes 135176 | tf_op jit(solution)/shard_map/ppermute | solution.py:225
  18.3 8.2 %collective-permute-start.4 = (f32[11,8,128]{2,1,0:T(8,128)S(1)}, f32[11,8,128]{2,1,0:T(8,128)S(1)}, u32[]{:S(2)}, u32[]{:S(2)}) collective-permute-start(f32[11,8,128]{2,1,0:T(8,128)S(1)} %get-tuple-element.10), channel_id=1, source_target_pairs={{0,1},{1,2},{2,3},{3,4},{4,5},{5,6},{6,7},{7,0},{8,9},{9,10},{10,1... | collective-permute-start | bytes 135176 | tf_op jit(solution)/shard_map/ppermute | solution.py:225
where the time goes:
time: 83.9 us; the launch traced here: 83.8 us
  blocking collectives  38.6 us (46%)
  Pallas kernels  17.3 us (21%)
  starting transfers between devices  15.6 us (19%)
  waiting for transfers between devices  9.18 us (11%)
  local copies, waits for them, and re-layouts  2.87 us (3%)
    all_to_all x1, blocking collectives, shards(): lax.all_to_all(sent.reshape(DEVICES, SLOTS, PLANES * N4), ('gx', 'gy'), s...  38.6 us
    pallas_call x1, Pallas kernels, shards(): pl.pallas_call(advance, out_shape=jax.ShapeDtypeStruct((DEVICES * SLOTS,...  17.3 us
    ppermute x6, starting transfers between devices, ring(): lax.ppermute(values, axis, [(i, (i + shift) % count) for i in range(count)])  15.6 us
    ppermute x6, waiting for transfers between devices, ring(): lax.ppermute(values, axis, [(i, (i + shift) % count) for i in range(count)])  9.18 us
  transfers between devices with their start and end apart: 6, of which 2 were waited for; matrix products, arithmetic and copies ran while one was open for 0% of the time, Pallas kernels for 0%

commit v1 on v0

--- a/solution.py
+++ b/solution.py
@@ -18,17 +18,20 @@
 LANES = 128
 SLOTS = 16
 OLD0 = 11
-PAD = 8
-ALL = ROWS + 2 * PAD
-FIRST = 4
+FACE = 8
+REACH = 4
+FIRST = 8
+OWN = FIRST + REACH
 GROUPS = 9
+WORK = 8 * GROUPS
+ALL = WORK + 2 * FIRST
 BLOCK = 512
 
 
 def advance(
     params, owner, prob, row_low, row_high, plane_low, plane_high, corner_low, corner_high, sent,
     u0, u1, u2, u3, xb, onehot, prefix, ones,
-    t_r0, t_f1, t_r1, t_d, t_r2, t_f2, t_f3, t_n, t_mask, target,
+    t_r0, t_f1, t_r1, t_d, t_r2, t_f2, t_f3, t_n, t_mask, target, by_one, even, odd,
 ):
     gx = lax.axis_index("gx")
     gy = lax.axis_index("gy")
@@ -58,7 +61,7 @@
 
     steps = [time_step / j for j in (4.0, 3.0, 2.0, 1.0)]
 
-    n1 = (gx * ROWS - PAD + LATTICE[1] + lax.broadcasted_iota(jnp.int32, (ALL, LANES), 0)) & (LATTICE[1] - 1)
+    n1 = (gx * ROWS - OWN + LATTICE[1] + lax.broadcasted_iota(jnp.int32, (ALL, LANES), 0)) & (LATTICE[1] - 1)
     rise_0 = rise(0, frac(n1, 1))
     leave_1 = rise_0 + fall(1, frac(n1, 1))
     fall_1 = fall(1, frac((n1 + 1) & (LATTICE[1] - 1), 1))
@@ -106,22 +109,21 @@
             t_n[q, n0, 3] = in_0
         return 0
 
-    lax.fori_loop(0, N0 - 1, species_zero, 0)
+    lax.fori_loop(0, N0, species_zero, 0)
 
     zero = jnp.zeros((ALL, LANES), F32)
     for t in range(4):
         for u, ks in (
-            (u0, (0, 12, 13, 14, 15, 16)), (u1, (0, 13, 14)), (u2, (0, 14, 15)), (u3, (0, 15, 16))
+            (u0, (0, 12, 13, 14, 15, 16)), (u1, (0, 13, 14, 15)), (u2, (0, 15)), (u3, (0, 15, 16, 17))
         ):
             for k in ks:
                 u[t, k] = zero
-    xb[pl.ds((N0 - 1) * ROWS, ROWS), :] = jnp.zeros((ROWS, 4 * LANES), BF16)
-
     prefix[...] = jnp.where(
         lax.broadcasted_iota(jnp.int32, (128, 128), 0) < lax.broadcasted_iota(jnp.int32, (128, 128), 1), 1.0, 0.0
     ).astype(BF16)
     ones[...] = jnp.ones((128, 128), BF16)
     running = jnp.zeros((DEVICES, 128), F32)
+    ranks = []
     peer = lax.broadcasted_iota(jnp.int32, (DEVICES, 128), 0)
     for b in range(8):
         part = owner[:, pl.ds(b * 128, 128)]
@@ -130,16 +132,24 @@
         count = running + jnp.dot(hit16, prefix[...], preferred_element_type=F32)
         running = running + jnp.dot(hit16, ones[...], preferred_element_type=F32)
         rank = jnp.sum(hit * count, axis=0, keepdims=True)
-        target[:, pl.ds(b * 128, 128)] = part.astype(F32) * float(SLOTS) + rank
-
-    def one_hot(i, _):
-        row = lax.broadcasted_iota(jnp.int32, (32, 1024), 0) + i * 32
-        onehot[pl.ds(pl.multiple_of(i * 32, 32), 32), :] = jnp.where(
-            row.astype(F32) == target[...], 1.0, 0.0
-        ).astype(BF16)
-        return 0
-
-    lax.fori_loop(0, DEVICES * SLOTS // 32, one_hot, 0)
+        ranks.append(rank)
+
+    slot = lax.broadcasted_iota(jnp.int32, (SLOTS, 1024), 0).astype(F32)
+    at_slot = jnp.where(slot == jnp.concatenate(ranks, axis=1), 1.0, 0.0).astype(BF16)
+    owners = jnp.broadcast_to(owner[...].astype(F32), (SLOTS, 1024)).astype(BF16)
+
+    def one_hot(o, now):
+        onehot[pl.ds(pl.multiple_of(o * SLOTS, SLOTS), SLOTS), :] = jnp.where(
+            owners == now, at_slot, jnp.zeros_like(at_slot)
+        )
+        return now + jnp.ones_like(now)
+
+    lax.fori_loop(0, DEVICES, one_hot, jnp.zeros((SLOTS, 1024), BF16))
+
+    source = lax.broadcasted_iota(jnp.int32, (2 * LANES, 2 * LANES), 0) & (LANES - 1)
+    column = lax.broadcasted_iota(jnp.int32, (2 * LANES, 2 * LANES), 1)
+    wanted = jnp.where(column < LANES, column + LANES - 1, column + 1) & (LANES - 1)
+    by_one[...] = jnp.where(source == wanted, 1.0, 0.0).astype(BF16)
 
     def prepare(n0, _):
         def put(t, row, count, values):
@@ -148,13 +158,13 @@
 
         for h in range(2):
             lanes = pl.ds(h * LANES, LANES)
-            put(1 + h, 0, PAD, row_low[n0, :, lanes])
-            put(1 + h, PAD + ROWS, PAD, row_high[n0, :, lanes])
-            put(1 + h, PAD, ROWS, prob[n0, :, lanes])
+            put(1 + h, FIRST, REACH, row_low[n0, pl.ds(FACE - REACH, REACH), lanes])
+            put(1 + h, OWN + ROWS, REACH, row_high[n0, pl.ds(0, REACH), lanes])
+            put(1 + h, OWN, ROWS, prob[n0, :, lanes])
         for t, plane, corner in ((0, plane_low, corner_low), (3, plane_high, corner_high)):
-            put(t, PAD, ROWS, plane[n0])
-            put(t, 0, PAD, corner[n0])
-            put(t, PAD + ROWS, 4, corner[n0, pl.ds(0, 4), :])
+            put(t, FIRST, REACH, corner[n0, pl.ds(REACH, REACH), :])
+            put(t, OWN + ROWS, REACH, corner[n0, pl.ds(0, REACH), :])
+            put(t, OWN, ROWS, plane[n0])
         return 0
 
     lax.fori_loop(0, OLD0, prepare, 0)
@@ -163,14 +173,24 @@
     first_plane = lane < N4
     last_plane = lane >= LANES - N4
 
+    def shift(q, src, n0, moved):
+        tiles = (1, 2) if q == 3 else range(4)
+        rows = jnp.concatenate([src[a, n0 + 1, pl.ds(FIRST, WORK), :] for a in tiles], axis=0)
+        high = rows.astype(BF16)
+        low = (rows - high.astype(F32)).astype(BF16)
+        both = jnp.dot(jnp.concatenate([high, low], axis=1), by_one[...], preferred_element_type=F32)
+        count = pl.ds(0, rows.shape[0])
+        moved[0, count, :] = both[:, :LANES]
+        moved[1, count, :] = both[:, LANES:]
+
     def stage(q, src, dst):
         last = q == 3
 
-        def body(n0, _):
+        def update(n0, moved):
             r3, f0, l0, m0 = (t_n[q, n0, i] for i in range(4))
             kept = {1: [], 2: []}
             for g in range(8 if last else GROUPS):
-                row = 8 * g + (PAD if last else FIRST)
+                row = 8 * g + (OWN if last else FIRST)
                 rows = pl.ds(row, 8)
                 r0 = t_r0[q, rows, :] * m0
                 f1 = t_f1[q, rows, :]
@@ -188,7 +208,8 @@
                         + f1 * src[a, n0 + 1, pl.ds(row + 1, 8), :]
                     )
                     acc = acc + (t_r2[q, a] * from_below + t_f2[q, a] * from_above)
-                    acc = acc + (r3 * pltpu.roll(c, 1, 1) + t_f3[q] * pltpu.roll(c, LANES - 1, 1))
+                    place = pl.ds(WORK * (a - 1 if last else a) + row - FIRST, 8)
+                    acc = acc + (r3 * moved[0, place, :] + t_f3[q] * moved[1, place, :])
                     if last:
                         kept[a].append(acc)
                     else:
@@ -202,9 +223,17 @@
                         low = (pair - high.astype(F32)).astype(BF16)
                         dst[place, pl.ds((a - 1) * LANES, LANES)] = high
                         dst[place, pl.ds((a + 1) * LANES, LANES)] = low
+
+        def body(i, _):
+            n0 = 2 * i
+            shift(q, src, n0 + 1, odd)
+            update(n0, even)
+            shift(q, src, n0 + 2, even)
+            update(n0 + 1, odd)
             return 0
 
-        lax.fori_loop(0, 12 + q, body, 0)
+        shift(q, src, 0, even)
+        lax.fori_loop(0, (13 + q) // 2, body, 0)
 
     stage(0, u0, u1)
     stage(1, u1, u2)
@@ -229,8 +258,8 @@
     vmem = pltpu.VMEM
     field = probability[0]
     inner = field[:OLD0]
-    row_low = ring(inner[:, ROWS - PAD:], "gx", 1)
-    row_high = ring(inner[:, :PAD], "gx", -1)
+    row_low = ring(inner[:, ROWS - FACE:], "gx", 1)
+    row_high = ring(inner[:, :FACE], "gx", -1)
     plane_low = ring(inner[:, :, LANES:], "gy", 1)
     plane_high = ring(inner[:, :, :LANES], "gy", -1)
     corner = jnp.concatenate([row_high[:, :4], row_low[:, 4:]], axis=1)
@@ -246,10 +275,10 @@
         in_specs=[pl.BlockSpec(memory_space=pltpu.SMEM)] + [whole] * 8,
         out_specs=whole,
         scratch_shapes=[
-            vmem((4, N0 + 1, ALL, LANES), F32),
-            vmem((4, N0 + 1, ALL, LANES), F32),
-            vmem((4, N0 + 1, ALL, LANES), F32),
-            vmem((4, N0 + 1, ALL, LANES), F32),
+            vmem((4, N0 + 2, ALL, LANES), F32),
+            vmem((4, N0 + 2, ALL, LANES), F32),
+            vmem((4, N0 + 2, ALL, LANES), F32),
+            vmem((4, N0 + 2, ALL, LANES), F32),
             vmem((N0 * ROWS, 4 * LANES), BF16),
             vmem((DEVICES * SLOTS, N0 * ROWS), BF16),
             vmem((128, 128), BF16),
@@ -264,6 +293,9 @@
             vmem((4, N0, 4, 8, LANES), F32),
             vmem((4, ALL, LANES), F32),
             vmem((1, N0 * ROWS), F32),
+            vmem((2 * LANES, 2 * LANES), BF16),
+            vmem((2, 4 * WORK, LANES), F32),
+            vmem((2, 4 * WORK, LANES), F32),
         ],
         compiler_params=pltpu.CompilerParams(vmem_limit_bytes=40 * 1024 * 1024),
         name="advance",

time: 83.9 us -> 80.9 us (0.964)
  Pallas kernels: 17.3 us -> 14.4 us
    pallas_call x1, Pallas kernels: 17.3 us -> 14.4 us  [shards(): pl.pallas_call(advance, out_shape=jax.ShapeDtypeStruct((DEVICES * SLOTS,...]
where the time goes in v1:
time: 80.9 us; the launch traced here: 80.8 us
  blocking collectives  38.6 us (48%)
  starting transfers between devices  15.6 us (19%)
  Pallas kernels  14.4 us (18%)
  waiting for transfers between devices  9.18 us (11%)
  local copies, waits for them, and re-layouts  2.87 us (4%)
    all_to_all x1, blocking collectives, shards(): lax.all_to_all(sent.reshape(DEVICES, SLOTS, PLANES * N4), ('gx', 'gy'), s...  38.6 us
    ppermute x6, starting transfers between devices, ring(): lax.ppermute(values, axis, [(i, (i + shift) % count) for i in range(count)])  15.6 us
    pallas_call x1, Pallas kernels, shards(): pl.pallas_call(advance, out_shape=jax.ShapeDtypeStruct((DEVICES * SLOTS,...  14.4 us
    ppermute x6, waiting for transfers between devices, ring(): lax.ppermute(values, axis, [(i, (i + shift) % count) for i in range(count)])  9.18 us
  transfers between devices with their start and end apart: 6, of which 2 were waited for; matrix products, arithmetic and copies ran while one was open for 0% of the time, Pallas kernels for 0%

profile of v1, /device:TPU:0, one launch (start us, length us, event | category | flops | bytes accessed | tf_op | source)
XLA Modules:
  0.0 80.8 jit_solution(13336584825137461857)
XLA Ops:
  0.0 0.0 copy-start.3
  0.0 0.0 copy-start.1
  0.0 1.3 %slice_bitcast_fusion = f32[11,64,256]{2,1,0:T(8,128)S(1)} fusion(f32[1,16,64,256]{3,2,1,0:T(8,128)} %param.7), kind=kLoop, calls=%fused_computation | loop fusion | bytes 1441792 | tf_op jit(solution)/shard_map/slice | solution.py:260
  1.3 4.0 %collective-permute-start.1 = (f32[11,8,256]{2,1,0:T(8,128)S(1)}, f32[11,8,256]{2,1,0:T(8,128)S(1)}, u32[]{:S(2)}, u32[]{:S(2)}) collective-permute-start(f32[11,8,256]{2,1,0:T(8,128)S(1)} %get-tuple-element.7), channel_id=1, source_target_pairs={{0,120},{8,0},{16,8},{24,16},{32,24},{40,32},{48,40},{56,48},{64,5... | collective-permute-start | bytes 270344 | tf_op jit(solution)/shard_map/ppermute | solution.py:254
  5.3 0.0 collective-permute-start
  5.3 0.1 fusion.1
  5.4 5.8 %collective-permute-start.3 = (f32[11,64,128]{2,1,0:T(8,128)S(1)}, f32[11,64,128]{2,1,0:T(8,128)S(1)}, u32[]{:S(2)}, u32[]{:S(2)}) collective-permute-start(f32[11,64,128]{2,1,0:T(8,128)S(1)} %get-tuple-element.5), channel_id=1, source_target_pairs={{0,7},{1,0},{2,1},{3,2},{4,3},{5,4},{6,5},{7,6},{8,15},{9,8},{10,9... | collective-permute-start | bytes 1081352 | tf_op jit(solution)/shard_map/ppermute | solution.py:254
  11.2 0.0 collective-permute-start.2
  11.2 0.0 collective-permute-done.1.row_high
  11.2 1.2 %collective-permute-done.row_low = f32[11,8,256]{2,1,0:T(8,128)S(1)} collective-permute-done((f32[11,8,256]{2,1,0:T(8,128)S(1)}, f32[11,8,256]{2,1,0:T(8,128)S(1)}, u32[]{:S(2)}, u32[]{:S(2)}) %collective-permute-start) | collective-permute-done | bytes 90144 | tf_op jit(solution)/shard_map/ppermute | solution.py:254
  12.5 5.8 %collective-permute-start.5 = (f32[11,8,128]{2,1,0:T(8,128)S(1)}, f32[11,8,128]{2,1,0:T(8,128)S(1)}, u32[]{:S(2)}, u32[]{:S(2)}) collective-permute-start(f32[11,8,128]{2,1,0:T(8,128)S(1)} %get-tuple-element.9), channel_id=1, source_target_pairs={{0,7},{1,0},{2,1},{3,2},{4,3},{5,4},{6,5},{7,6},{8,15},{9,8},{10,9... | collective-permute-start | bytes 135176 | tf_op jit(solution)/shard_map/ppermute | solution.py:254
  18.3 0.0 collective-permute-start.4
  18.3 0.0 copy-done.2
  18.3 0.1 convert_element_type.19
  18.4 0.0 copy-done.4
  18.4 0.1 concatenate.6.params
  18.5 8.0 %collective-permute-done.5.corner_high = f32[11,8,128]{2,1,0:T(8,128)S(1)} collective-permute-done((f32[11,8,128]{2,1,0:T(8,128)S(1)}, f32[11,8,128]{2,1,0:T(8,128)S(1)}, u32[]{:S(2)}, u32[]{:S(2)}) %collective-permute-start.5) | collective-permute-done | bytes 45088 | tf_op jit(solution)/shard_map/ppermute | solution.py:254
  26.5 0.0 collective-permute-done.4.corner_low
  26.5 0.0 collective-permute-done.3.plane_high
  26.5 0.0 collective-permute-done.2.plane_low
  26.5 0.0 copy-done
  26.5 14.4 %advance.1 = f32[2048,256]{1,0:T(8,128)S(1)} custom-call(f32[56]{0:T(128)S(1)} %concatenate.6.params, s32[1,1024]{1,0:T(1,128)S(1)} %bitcast.10, f32[16,64,256]{2,1,0:T(8,128)S(1)} %bitcast.9, f32[11,8,256]{2,1,0:T(8,128)S(1)} %collective-permute-done.row_low, f32[11,8,256]{2,1,0:T(8,128)S(1)} %collective-permute-done.1.row_high, ...), custom_call_target="tpu_custom_call" | custom-call | tf_op jit(solution)/shard_map/advance/pallas_call | solution.py:272
  40.9 38.6 %all_to_all.5 = f32[128,16,256]{2,1,0:T(8,128)S(1)} all-to-all(f32[128,16,256]{2,1,0:T(8,128)S(1)} %bitcast.8), channel_id=1, replica_groups=mesh['gx'=16,'gy'=8] {'gx','gy'}, dimensions={0} | all-to-all | bytes 4194304 | tf_op jit(solution)/shard_map/all_to_all | solution.py:306
  79.5 1.3 %copy.9 = f32[1,128,16,256]{3,2,1,0:T(8,128)} copy(f32[1,128,16,256]{3,2,1,0:T(8,128)S(1)} %bitcast.11) | data formatting | bytes 4194304
  (16 shorter events, 0.1 us)
Async XLA Ops:
  0.0 26.5 %copy-start = (f32[1,16,64,256]{3,2,1,0:T(8,128)S(1)}, f32[1,16,64,256]{3,2,1,0:T(8,128)}, u32[]{:S(2)}) copy-start(f32[1,16,64,256]{3,2,1,0:T(8,128)} %param.7) | copy-start | bytes 3145732
  0.0 18.3 %copy-start.2 = (s32[8,4]{0,1:T(4,128)S(1)}, s32[8,4]{0,1:T(4,128)}, u32[]{:S(2)}) copy-start(s32[8,4]{0,1:T(4,128)} %param.12) | copy-start | bytes 388
  0.0 18.3 %copy-start.5 = (s32[4]{0:T(128)S(1)}, s32[4]{0:T(128)}, u32[]{:S(2)}) copy-start(s32[4]{0:T(128)} %param.8) | copy-start | bytes 52
  0.0 18.3 %copy-start.6 = (s32[4]{0:T(128)S(1)}, s32[4]{0:T(128)}, u32[]{:S(2)}) copy-start(s32[4]{0:T(128)} %param.9) | copy-start | bytes 52
  0.0 18.4 %copy-start.4 = (f32[8]{0:T(128)S(1)}, f32[8]{0:T(128)}, u32[]{:S(2)}) copy-start(f32[8]{0:T(128)} %param.11) | copy-start | bytes 100
  0.0 18.4 %copy-start.3 = (f32[8]{0:T(128)S(1)}, f32[8]{0:T(128)}, u32[]{:S(2)}) copy-start(f32[8]{0:T(128)} %param.10) | copy-start | bytes 100
  0.0 26.5 %copy-start.1 = (s32[1,1,1024,1]{2,3,1,0:T(1,128)S(1)}, s32[1,1,1024,1]{2,3,1,0:T(1,128)}, u32[]{:S(2)}) copy-start(s32[1,1,1024,1]{2,3,1,0:T(1,128)} %param.13) | copy-start | bytes 12292
  1.3 9.9 %collective-permute-start.1 = (f32[11,8,256]{2,1,0:T(8,128)S(1)}, f32[11,8,256]{2,1,0:T(8,128)S(1)}, u32[]{:S(2)}, u32[]{:S(2)}) collective-permute-start(f32[11,8,256]{2,1,0:T(8,128)S(1)} %get-tuple-element.7), channel_id=1, source_target_pairs={{0,120},{8,0},{16,8},{24,16},{32,24},{40,32},{48,40},{56,48},{64,5... | collective-permute-start | bytes 270344 | tf_op jit(solution)/shard_map/ppermute | solution.py:254
  5.3 7.1 %collective-permute-start = (f32[11,8,256]{2,1,0:T(8,128)S(1)}, f32[11,8,256]{2,1,0:T(8,128)S(1)}, u32[]{:S(2)}, u32[]{:S(2)}) collective-permute-start(f32[11,8,256]{2,1,0:T(8,128)S(1)} %get-tuple-element.8), channel_id=1, source_target_pairs={{0,8},{8,16},{16,24},{24,32},{32,40},{40,48},{48,56},{56,64},{64,7... | collective-permute-start | bytes 270344 | tf_op jit(solution)/shard_map/ppermute | solution.py:254
  5.4 21.1 %collective-permute-start.3 = (f32[11,64,128]{2,1,0:T(8,128)S(1)}, f32[11,64,128]{2,1,0:T(8,128)S(1)}, u32[]{:S(2)}, u32[]{:S(2)}) collective-permute-start(f32[11,64,128]{2,1,0:T(8,128)S(1)} %get-tuple-element.5), channel_id=1, source_target_pairs={{0,7},{1,0},{2,1},{3,2},{4,3},{5,4},{6,5},{7,6},{8,15},{9,8},{10,9... | collective-permute-start | bytes 1081352 | tf_op jit(solution)/shard_map/ppermute | solution.py:254
  11.2 15.3 %collective-permute-start.2 = (f32[11,64,128]{2,1,0:T(8,128)S(1)}, f32[11,64,128]{2,1,0:T(8,128)S(1)}, u32[]{:S(2)}, u32[]{:S(2)}) collective-permute-start(f32[11,64,128]{2,1,0:T(8,128)S(1)} %get-tuple-element.6), channel_id=1, source_target_pairs={{0,1},{1,2},{2,3},{3,4},{4,5},{5,6},{6,7},{7,0},{8,9},{9,10},{10,1... | collective-permute-start | bytes 1081352 | tf_op jit(solution)/shard_map/ppermute | solution.py:254
  12.5 14.0 %collective-permute-start.5 = (f32[11,8,128]{2,1,0:T(8,128)S(1)}, f32[11,8,128]{2,1,0:T(8,128)S(1)}, u32[]{:S(2)}, u32[]{:S(2)}) collective-permute-start(f32[11,8,128]{2,1,0:T(8,128)S(1)} %get-tuple-element.9), channel_id=1, source_target_pairs={{0,7},{1,0},{2,1},{3,2},{4,3},{5,4},{6,5},{7,6},{8,15},{9,8},{10,9... | collective-permute-start | bytes 135176 | tf_op jit(solution)/shard_map/ppermute | solution.py:254
  18.3 8.2 %collective-permute-start.4 = (f32[11,8,128]{2,1,0:T(8,128)S(1)}, f32[11,8,128]{2,1,0:T(8,128)S(1)}, u32[]{:S(2)}, u32[]{:S(2)}) collective-permute-start(f32[11,8,128]{2,1,0:T(8,128)S(1)} %get-tuple-element.10), channel_id=1, source_target_pairs={{0,1},{1,2},{2,3},{3,4},{4,5},{5,6},{6,7},{7,0},{8,9},{9,10},{10,1... | collective-permute-start | bytes 135176 | tf_op jit(solution)/shard_map/ppermute | solution.py:254

commit v2 on v1

--- a/solution.py
+++ b/solution.py
@@ -28,10 +28,8 @@
 BLOCK = 512
 
 
-def advance(
-    params, owner, prob, row_low, row_high, plane_low, plane_high, corner_low, corner_high, sent,
-    u0, u1, u2, u3, xb, onehot, prefix, ones,
-    t_r0, t_f1, t_r1, t_d, t_r2, t_f2, t_f3, t_n, t_mask, target, by_one, even, odd,
+def prepare_tables(
+    params, owner, t_r0, t_f1, t_r1, t_d, t_r2, t_f2, t_f3, t_n, t_mask, by_one, onehot, prefix, ones
 ):
     gx = lax.axis_index("gx")
     gy = lax.axis_index("gy")
@@ -111,13 +109,6 @@
 
     lax.fori_loop(0, N0, species_zero, 0)
 
-    zero = jnp.zeros((ALL, LANES), F32)
-    for t in range(4):
-        for u, ks in (
-            (u0, (0, 12, 13, 14, 15, 16)), (u1, (0, 13, 14, 15)), (u2, (0, 15)), (u3, (0, 15, 16, 17))
-        ):
-            for k in ks:
-                u[t, k] = zero
     prefix[...] = jnp.where(
         lax.broadcasted_iota(jnp.int32, (128, 128), 0) < lax.broadcasted_iota(jnp.int32, (128, 128), 1), 1.0, 0.0
     ).astype(BF16)
@@ -151,6 +142,19 @@
     wanted = jnp.where(column < LANES, column + LANES - 1, column + 1) & (LANES - 1)
     by_one[...] = jnp.where(source == wanted, 1.0, 0.0).astype(BF16)
 
+
+def advance(
+    prob, row_low, row_high, plane_low, plane_high, corner_low, corner_high,
+    t_r0, t_f1, t_r1, t_d, t_r2, t_f2, t_f3, t_n, t_mask, by_one, onehot, sent,
+    u0, u1, u2, u3, xb, even, odd,
+):
+    zero = jnp.zeros((ALL, LANES), F32)
+    for t in range(4):
+        for u, ks in (
+            (u0, (0, 12, 13, 14, 15, 16, 17)), (u1, (0, 13, 14, 15, 16, 17)), (u2, (0, 17)), (u3, (0, 17))
+        ):
+            for k in ks:
+                u[t, k] = zero
     def prepare(n0, _):
         def put(t, row, count, values):
             rows = pl.ds(row, count)
@@ -175,65 +179,78 @@
 
     def shift(q, src, n0, moved):
         tiles = (1, 2) if q == 3 else range(4)
-        rows = jnp.concatenate([src[a, n0 + 1, pl.ds(FIRST, WORK), :] for a in tiles], axis=0)
-        high = rows.astype(BF16)
-        low = (rows - high.astype(F32)).astype(BF16)
-        both = jnp.dot(jnp.concatenate([high, low], axis=1), by_one[...], preferred_element_type=F32)
-        count = pl.ds(0, rows.shape[0])
-        moved[0, count, :] = both[:, :LANES]
-        moved[1, count, :] = both[:, LANES:]
+        f3 = t_f3[q]
+        for k in range(2):
+            r3 = t_n[q, n0 + k, 0]
+            rows = jnp.concatenate([src[a, n0 + k + 1, pl.ds(FIRST, WORK), :] for a in tiles], axis=0)
+            high = rows.astype(BF16)
+            low = (rows - high.astype(F32)).astype(BF16)
+            both = jnp.dot(jnp.concatenate([high, low], axis=1), by_one[...], preferred_element_type=F32)
+            both = both.reshape(-1, 8, 2 * LANES)
+            flow = r3[None] * both[:, :, :LANES] + f3[None] * both[:, :, LANES:]
+            moved[k, pl.ds(0, rows.shape[0]), :] = flow.reshape(rows.shape)
 
     def stage(q, src, dst):
         last = q == 3
 
         def update(n0, moved):
-            r3, f0, l0, m0 = (t_n[q, n0, i] for i in range(4))
-            kept = {1: [], 2: []}
+            pair = range(2)
+            f0, l0, m0 = ([t_n[q, n0 + k, i] for k in pair] for i in (1, 2, 3))
+            r2 = [t_r2[q, a] for a in range(4)]
+            f2 = [t_f2[q, a] for a in range(4)]
+            kept = {(k, a): [] for k in pair for a in (1, 2)}
             for g in range(8 if last else GROUPS):
                 row = 8 * g + (OWN if last else FIRST)
                 rows = pl.ds(row, 8)
-                r0 = t_r0[q, rows, :] * m0
+                r0 = t_r0[q, rows, :]
                 f1 = t_f1[q, rows, :]
-                centre = [src[a, n0 + 1, rows, :] for a in range(4)]
-                up = [pltpu.roll(c, N4, 1) for c in centre]
-                down = [pltpu.roll(c, LANES - N4, 1) for c in centre]
+                r0 = [r0 * m0[k] for k in pair]
+                centre = [[src[a, n0 + k + 1, rows, :] for a in range(4)] for k in pair]
+                up = [[pltpu.roll(c, N4, 1) for c in centre[k]] for k in pair]
+                down = [[pltpu.roll(c, LANES - N4, 1) for c in centre[k]] for k in pair]
                 for a in ((1, 2) if last else range(4)):
-                    c = centre[a]
-                    from_below = jnp.where(first_plane, up[a - 1], up[a]) if a > 0 else up[a]
-                    from_above = jnp.where(last_plane, down[a + 1], down[a]) if a < 3 else down[a]
-                    acc = u0[a, n0 + 1, rows, :] + (t_d[q, a, rows, :] + l0) * c
-                    acc = acc + (r0 * src[a, n0, rows, :] + f0 * src[a, n0 + 2, rows, :])
-                    acc = acc + (
-                        t_r1[q, a, rows, :] * src[a, n0 + 1, pl.ds(row - 1, 8), :]
-                        + f1 * src[a, n0 + 1, pl.ds(row + 1, 8), :]
-                    )
-                    acc = acc + (t_r2[q, a] * from_below + t_f2[q, a] * from_above)
+                    before = [src[a, n0, rows, :], centre[0][a]]
+                    after = [centre[1][a], src[a, n0 + 3, rows, :]]
+                    d = t_d[q, a, rows, :]
+                    r1 = t_r1[q, a, rows, :]
                     place = pl.ds(WORK * (a - 1 if last else a) + row - FIRST, 8)
-                    acc = acc + (r3 * moved[0, place, :] + t_f3[q] * moved[1, place, :])
-                    if last:
-                        kept[a].append(acc)
-                    else:
-                        dst[a, n0 + 1, rows, :] = acc
+                    for k in pair:
+                        c = centre[k][a]
+                        from_below = jnp.where(first_plane, up[k][a - 1], up[k][a]) if a > 0 else up[k][a]
+                        from_above = jnp.where(last_plane, down[k][a + 1], down[k][a]) if a < 3 else down[k][a]
+                        acc = u0[a, n0 + k + 1, rows, :] + (d + l0[k]) * c
+                        acc = acc + (r0[k] * before[k] + f0[k] * after[k])
+                        acc = acc + (
+                            r1 * src[a, n0 + k + 1, pl.ds(row - 1, 8), :]
+                            + f1 * src[a, n0 + k + 1, pl.ds(row + 1, 8), :]
+                        )
+                        acc = acc + (r2[a] * from_below + f2[a] * from_above)
+                        acc = acc + moved[k, place, :]
+                        if last:
+                            kept[k, a].append(acc)
+                        else:
+                            dst[a, n0 + k + 1, rows, :] = acc
                 if last and g % 2 == 1:
-                    place = pl.ds(pl.multiple_of(n0 * ROWS + 8 * (g - 1), 16), 16)
-                    for a in (1, 2):
-                        pair = jnp.concatenate(kept[a], axis=0)
-                        kept[a] = []
-                        high = pair.astype(BF16)
-                        low = (pair - high.astype(F32)).astype(BF16)
-                        dst[place, pl.ds((a - 1) * LANES, LANES)] = high
-                        dst[place, pl.ds((a + 1) * LANES, LANES)] = low
+                    for k in pair:
+                        place = pl.ds(pl.multiple_of((n0 + k) * ROWS + 8 * (g - 1), 16), 16)
+                        for a in (1, 2):
+                            both = jnp.concatenate(kept[k, a], axis=0)
+                            kept[k, a] = []
+                            high = both.astype(BF16)
+                            low = (both - high.astype(F32)).astype(BF16)
+                            dst[place, pl.ds((a - 1) * LANES, LANES)] = high
+                            dst[place, pl.ds((a + 1) * LANES, LANES)] = low
 
         def body(i, _):
-            n0 = 2 * i
-            shift(q, src, n0 + 1, odd)
+            n0 = 4 * i
+            shift(q, src, n0 + 2, odd)
             update(n0, even)
-            shift(q, src, n0 + 2, even)
-            update(n0 + 1, odd)
+            shift(q, src, jnp.minimum(n0 + 4, N0 - 2), even)
+            update(n0 + 2, odd)
             return 0
 
         shift(q, src, 0, even)
-        lax.fori_loop(0, (13 + q) // 2, body, 0)
+        lax.fori_loop(0, 3 if q == 0 else 4, body, 0)
 
     stage(0, u0, u1)
     stage(1, u1, u2)
@@ -269,10 +286,33 @@
         [extent.astype(F32), slab_width.astype(F32), rate_const, hill_const, stoichiometry.T.reshape(32).astype(F32)]
     )
     whole = pl.BlockSpec(memory_space=pltpu.VMEM)
+    tables = [
+        ((4, ALL, LANES), F32),
+        ((4, ALL, LANES), F32),
+        ((4, 4, ALL, LANES), F32),
+        ((4, 4, ALL, LANES), F32),
+        ((4, 4, 8, LANES), F32),
+        ((4, 4, 8, LANES), F32),
+        ((4, 8, LANES), F32),
+        ((4, N0, 4, 8, LANES), F32),
+        ((4, ALL, LANES), F32),
+        ((2 * LANES, 2 * LANES), BF16),
+        ((DEVICES * SLOTS, N0 * ROWS), BF16),
+    ]
+    made = pl.pallas_call(
+        prepare_tables,
+        out_shape=[jax.ShapeDtypeStruct(*table) for table in tables],
+        in_specs=[pl.BlockSpec(memory_space=pltpu.SMEM), whole],
+        out_specs=[whole] * len(tables),
+        scratch_shapes=[vmem((128, 128), BF16), vmem((128, 128), BF16)],
+        compiler_params=pltpu.CompilerParams(vmem_limit_bytes=12 * 1024 * 1024),
+        cost_estimate=pl.CostEstimate(flops=10_000_000, bytes_accessed=16_000_000, transcendentals=0),
+        name="prepare_tables",
+    )(params, new_owner.reshape(1, N0 * ROWS))
     sent = pl.pallas_call(
         advance,
         out_shape=jax.ShapeDtypeStruct((DEVICES * SLOTS, PLANES * N4), F32),
-        in_specs=[pl.BlockSpec(memory_space=pltpu.SMEM)] + [whole] * 8,
+        in_specs=[whole] * (7 + len(tables)),
         out_specs=whole,
         scratch_shapes=[
             vmem((4, N0 + 2, ALL, LANES), F32),
@@ -280,29 +320,12 @@
             vmem((4, N0 + 2, ALL, LANES), F32),
             vmem((4, N0 + 2, ALL, LANES), F32),
             vmem((N0 * ROWS, 4 * LANES), BF16),
-            vmem((DEVICES * SLOTS, N0 * ROWS), BF16),
-            vmem((128, 128), BF16),
-            vmem((128, 128), BF16),
-            vmem((4, ALL, LANES), F32),
-            vmem((4, ALL, LANES), F32),
-            vmem((4, 4, ALL, LANES), F32),
-            vmem((4, 4, ALL, LANES), F32),
-            vmem((4, 4, 8, LANES), F32),
-            vmem((4, 4, 8, LANES), F32),
-            vmem((4, 8, LANES), F32),
-            vmem((4, N0, 4, 8, LANES), F32),
-            vmem((4, ALL, LANES), F32),
-            vmem((1, N0 * ROWS), F32),
-            vmem((2 * LANES, 2 * LANES), BF16),
             vmem((2, 4 * WORK, LANES), F32),
             vmem((2, 4 * WORK, LANES), F32),
         ],
-        compiler_params=pltpu.CompilerParams(vmem_limit_bytes=40 * 1024 * 1024),
+        compiler_params=pltpu.CompilerParams(vmem_limit_bytes=32 * 1024 * 1024),
         name="advance",
-    )(
-        params, new_owner.reshape(1, N0 * ROWS), field, row_low, row_high, plane_low, plane_high,
-        corner_low, corner_high,
-    )
+    )(field, row_low, row_high, plane_low, plane_high, corner_low, corner_high, *made)
     moved = lax.all_to_all(
         sent.reshape(DEVICES, SLOTS, PLANES * N4), ("gx", "gy"), split_axis=0, concat_axis=0, tiled=True
     )

time: 80.9 us -> 78.2 us (0.967)
  waiting for transfers between devices: 9.18 us -> 6.91 us
    pallas_call x1, Pallas kernels: 14.4 us -> 11.6 us  [shards(): pl.pallas_call(advance, out_shape=jax.ShapeDtypeStruct((DEVICES * SLOTS,...]
    ppermute x6, waiting for transfers between devices: 9.18 us -> 6.91 us  [ring(): lax.ppermute(values, axis, [(i, (i + shift) % count) for i in range(count)])]
    pallas_call x0 -> x1, Pallas kernels: none -> 2.27 us  [shards(): pl.pallas_call(prepare_tables, out_shape=[jax.ShapeDtypeStruct(*table) fo...]
  transfers between devices with their start and end apart: 6 -> 6, of which waited for: 2 -> 2; matrix products, arithmetic and copies ran while one was open for 0% -> 0% of each run, Pallas kernels for 0% -> 3%
where the time goes in v2:
time: 78.2 us; the launch traced here: 78.1 us
  blocking collectives  38.6 us (49%)
  starting transfers between devices  15.6 us (20%)
  Pallas kernels  13.9 us (18%)
  waiting for transfers between devices  6.91 us (9%)
  local copies, waits for them, and re-layouts  2.87 us (4%)
    all_to_all x1, blocking collectives, shards(): lax.all_to_all(sent.reshape(DEVICES, SLOTS, PLANES * N4), ('gx', 'gy'), s...  38.6 us
    ppermute x6, starting transfers between devices, ring(): lax.ppermute(values, axis, [(i, (i + shift) % count) for i in range(count)])  15.6 us
    pallas_call x1, Pallas kernels, shards(): pl.pallas_call(advance, out_shape=jax.ShapeDtypeStruct((DEVICES * SLOTS,...  11.6 us
    ppermute x6, waiting for transfers between devices, ring(): lax.ppermute(values, axis, [(i, (i + shift) % count) for i in range(count)])  6.91 us
    pallas_call x1, Pallas kernels, shards(): pl.pallas_call(prepare_tables, out_shape=[jax.ShapeDtypeStruct(*table) fo...  2.27 us
  transfers between devices with their start and end apart: 6, of which 2 were waited for; matrix products, arithmetic and copies ran while one was open for 0% of the time, Pallas kernels for 3%

profile of v2, /device:TPU:0, one launch (start us, length us, event | category | flops | bytes accessed | tf_op | source)
XLA Modules:
  0.0 78.1 jit_solution(16249538979782328978)
XLA Ops:
  0.0 0.0 copy-start.3
  0.0 0.0 copy-start.1
  0.0 1.3 %slice_bitcast_fusion = f32[11,64,256]{2,1,0:T(8,128)S(1)} fusion(f32[1,16,64,256]{3,2,1,0:T(8,128)} %param.7), kind=kLoop, calls=%fused_computation | loop fusion | bytes 1441792 | tf_op jit(solution)/shard_map/slice | solution.py:277
  1.3 4.0 %collective-permute-start.1 = (f32[11,8,256]{2,1,0:T(8,128)S(1)}, f32[11,8,256]{2,1,0:T(8,128)S(1)}, u32[]{:S(2)}, u32[]{:S(2)}) collective-permute-start(f32[11,8,256]{2,1,0:T(8,128)S(1)} %get-tuple-element.29), channel_id=1, source_target_pairs={{0,120},{8,0},{16,8},{24,16},{32,24},{40,32},{48,40},{56,48},{64,5... | collective-permute-start | bytes 270344 | tf_op jit(solution)/shard_map/ppermute | solution.py:271
  5.3 0.0 collective-permute-start
  5.3 0.1 fusion.1
  5.4 5.8 %collective-permute-start.3 = (f32[11,64,128]{2,1,0:T(8,128)S(1)}, f32[11,64,128]{2,1,0:T(8,128)S(1)}, u32[]{:S(2)}, u32[]{:S(2)}) collective-permute-start(f32[11,64,128]{2,1,0:T(8,128)S(1)} %get-tuple-element.27), channel_id=1, source_target_pairs={{0,7},{1,0},{2,1},{3,2},{4,3},{5,4},{6,5},{7,6},{8,15},{9,8},{10,9... | collective-permute-start | bytes 1081352 | tf_op jit(solution)/shard_map/ppermute | solution.py:271
  11.2 0.0 collective-permute-start.2
  11.2 0.0 collective-permute-done.1.row_high
  11.2 1.2 %collective-permute-done.row_low = f32[11,8,256]{2,1,0:T(8,128)S(1)} collective-permute-done((f32[11,8,256]{2,1,0:T(8,128)S(1)}, f32[11,8,256]{2,1,0:T(8,128)S(1)}, u32[]{:S(2)}, u32[]{:S(2)}) %collective-permute-start) | collective-permute-done | bytes 90144 | tf_op jit(solution)/shard_map/ppermute | solution.py:271
  12.5 5.8 %collective-permute-start.5 = (f32[11,8,128]{2,1,0:T(8,128)S(1)}, f32[11,8,128]{2,1,0:T(8,128)S(1)}, u32[]{:S(2)}, u32[]{:S(2)}) collective-permute-start(f32[11,8,128]{2,1,0:T(8,128)S(1)} %get-tuple-element.31), channel_id=1, source_target_pairs={{0,7},{1,0},{2,1},{3,2},{4,3},{5,4},{6,5},{7,6},{8,15},{9,8},{10,9... | collective-permute-start | bytes 135176 | tf_op jit(solution)/shard_map/ppermute | solution.py:271
  18.3 0.0 collective-permute-start.4
  18.3 0.0 copy-done.2
  18.3 0.1 convert_element_type.19
  18.4 0.0 copy-done.4
  18.4 0.1 concatenate.7.params
  18.5 2.3 %prepare_tables.1 = (f32[4,88,128]{2,1,0:T(8,128)S(1)}, f32[4,88,128]{2,1,0:T(8,128)S(1)}, f32[4,4,88,128]{3,2,1,0:T(8,128)S(1)}, f32[4,4,88,128]{3,2,1,0:T(8,12...) custom-call(f32[56]{0:T(128)S(1)} %concatenate.7.params, ...), custom_call_target="tpu_custom_call" | custom-call | flops 10000000 | bytes 16000000 | tf_op jit(solution)/shard_map/prepare_tables/pallas_call | solution.py:302
  20.8 5.7 %collective-permute-done.5.corner_high = f32[11,8,128]{2,1,0:T(8,128)S(1)} collective-permute-done((f32[11,8,128]{2,1,0:T(8,128)S(1)}, f32[11,8,128]{2,1,0:T(8,128)S(1)}, u32[]{:S(2)}, u32[]{:S(2)}) %collective-permute-start.5) | collective-permute-done | bytes 45088 | tf_op jit(solution)/shard_map/ppermute | solution.py:271
  26.5 0.0 collective-permute-done.4.corner_low
  26.5 0.0 collective-permute-done.3.plane_high
  26.5 0.0 collective-permute-done.2.plane_low
  26.5 11.6 %advance.1 = f32[2048,256]{1,0:T(8,128)S(1)} custom-call(f32[16,64,256]{2,1,0:T(8,128)S(1)} %bitcast.9, f32[11,8,256]{2,1,0:T(8,128)S(1)} %collective-permute-done.row_low, f32[11,8,256]{2,1,0:T(8,128)S(1)} %collective-permute-done.1.row_high, f32[11,64,128]{2,1,0:T(8,128)S(1)} %collective-permute-done.2.plane_low, ...), custom_call_target="tpu_custom_call" | custom-call | tf_op jit(solution)/shard_map/advance/pallas_call | solution.py:312
  38.2 38.6 %all_to_all.5 = f32[128,16,256]{2,1,0:T(8,128)S(1)} all-to-all(f32[128,16,256]{2,1,0:T(8,128)S(1)} %bitcast.8), channel_id=1, replica_groups=mesh['gx'=16,'gy'=8] {'gx','gy'}, dimensions={0} | all-to-all | bytes 4194304 | tf_op jit(solution)/shard_map/all_to_all | solution.py:329
  76.7 1.3 %copy.9 = f32[1,128,16,256]{3,2,1,0:T(8,128)} copy(f32[1,128,16,256]{3,2,1,0:T(8,128)S(1)} %bitcast.11) | data formatting | bytes 4194304
  (17 shorter events, 0.1 us)
Async XLA Ops:
  0.0 26.5 %copy-start = (f32[1,16,64,256]{3,2,1,0:T(8,128)S(1)}, f32[1,16,64,256]{3,2,1,0:T(8,128)}, u32[]{:S(2)}) copy-start(f32[1,16,64,256]{3,2,1,0:T(8,128)} %param.7) | copy-start | bytes 3145732
  0.0 18.3 %copy-start.2 = (s32[8,4]{0,1:T(4,128)S(1)}, s32[8,4]{0,1:T(4,128)}, u32[]{:S(2)}) copy-start(s32[8,4]{0,1:T(4,128)} %param.12) | copy-start | bytes 388
  0.0 18.3 %copy-start.5 = (s32[4]{0:T(128)S(1)}, s32[4]{0:T(128)}, u32[]{:S(2)}) copy-start(s32[4]{0:T(128)} %param.8) | copy-start | bytes 52
  0.0 18.3 %copy-start.6 = (s32[4]{0:T(128)S(1)}, s32[4]{0:T(128)}, u32[]{:S(2)}) copy-start(s32[4]{0:T(128)} %param.9) | copy-start | bytes 52
  0.0 18.4 %copy-start.4 = (f32[8]{0:T(128)S(1)}, f32[8]{0:T(128)}, u32[]{:S(2)}) copy-start(f32[8]{0:T(128)} %param.11) | copy-start | bytes 100
  0.0 18.4 %copy-start.3 = (f32[8]{0:T(128)S(1)}, f32[8]{0:T(128)}, u32[]{:S(2)}) copy-start(f32[8]{0:T(128)} %param.10) | copy-start | bytes 100
  0.0 18.5 %copy-start.1 = (s32[1,1,1024,1]{2,3,1,0:T(1,128)S(1)}, s32[1,1,1024,1]{2,3,1,0:T(1,128)}, u32[]{:S(2)}) copy-start(s32[1,1,1024,1]{2,3,1,0:T(1,128)} %param.13) | copy-start | bytes 12292
  1.3 9.9 %collective-permute-start.1 = (f32[11,8,256]{2,1,0:T(8,128)S(1)}, f32[11,8,256]{2,1,0:T(8,128)S(1)}, u32[]{:S(2)}, u32[]{:S(2)}) collective-permute-start(f32[11,8,256]{2,1,0:T(8,128)S(1)} %get-tuple-element.29), channel_id=1, source_target_pairs={{0,120},{8,0},{16,8},{24,16},{32,24},{40,32},{48,40},{56,48},{64,5... | collective-permute-start | bytes 270344 | tf_op jit(solution)/shard_map/ppermute | solution.py:271
  5.3 7.1 %collective-permute-start = (f32[11,8,256]{2,1,0:T(8,128)S(1)}, f32[11,8,256]{2,1,0:T(8,128)S(1)}, u32[]{:S(2)}, u32[]{:S(2)}) collective-permute-start(f32[11,8,256]{2,1,0:T(8,128)S(1)} %get-tuple-element.30), channel_id=1, source_target_pairs={{0,8},{8,16},{16,24},{24,32},{32,40},{40,48},{48,56},{56,64},{64,7... | collective-permute-start | bytes 270344 | tf_op jit(solution)/shard_map/ppermute | solution.py:271
  5.4 21.1 %collective-permute-start.3 = (f32[11,64,128]{2,1,0:T(8,128)S(1)}, f32[11,64,128]{2,1,0:T(8,128)S(1)}, u32[]{:S(2)}, u32[]{:S(2)}) collective-permute-start(f32[11,64,128]{2,1,0:T(8,128)S(1)} %get-tuple-element.27), channel_id=1, source_target_pairs={{0,7},{1,0},{2,1},{3,2},{4,3},{5,4},{6,5},{7,6},{8,15},{9,8},{10,9... | collective-permute-start | bytes 1081352 | tf_op jit(solution)/shard_map/ppermute | solution.py:271
  11.2 15.3 %collective-permute-start.2 = (f32[11,64,128]{2,1,0:T(8,128)S(1)}, f32[11,64,128]{2,1,0:T(8,128)S(1)}, u32[]{:S(2)}, u32[]{:S(2)}) collective-permute-start(f32[11,64,128]{2,1,0:T(8,128)S(1)} %get-tuple-element.28), channel_id=1, source_target_pairs={{0,1},{1,2},{2,3},{3,4},{4,5},{5,6},{6,7},{7,0},{8,9},{9,10},{10,1... | collective-permute-start | bytes 1081352 | tf_op jit(solution)/shard_map/ppermute | solution.py:271
  12.5 14.0 %collective-permute-start.5 = (f32[11,8,128]{2,1,0:T(8,128)S(1)}, f32[11,8,128]{2,1,0:T(8,128)S(1)}, u32[]{:S(2)}, u32[]{:S(2)}) collective-permute-start(f32[11,8,128]{2,1,0:T(8,128)S(1)} %get-tuple-element.31), channel_id=1, source_target_pairs={{0,7},{1,0},{2,1},{3,2},{4,3},{5,4},{6,5},{7,6},{8,15},{9,8},{10,9... | collective-permute-start | bytes 135176 | tf_op jit(solution)/shard_map/ppermute | solution.py:271
  18.3 8.2 %collective-permute-start.4 = (f32[11,8,128]{2,1,0:T(8,128)S(1)}, f32[11,8,128]{2,1,0:T(8,128)S(1)}, u32[]{:S(2)}, u32[]{:S(2)}) collective-permute-start(f32[11,8,128]{2,1,0:T(8,128)S(1)} %get-tuple-element.32), channel_id=1, source_target_pairs={{0,1},{1,2},{2,3},{3,4},{4,5},{5,6},{6,7},{7,0},{8,9},{9,10},{10,1... | collective-permute-start | bytes 135176 | tf_op jit(solution)/shard_map/ppermute | solution.py:271

commit v3 on v2

--- a/solution.py
+++ b/solution.py
@@ -29,10 +29,13 @@
 
 
 def prepare_tables(
-    params, owner, t_r0, t_f1, t_r1, t_d, t_r2, t_f2, t_f3, t_n, t_mask, by_one, onehot, prefix, ones
+    params, owner, last_rows, first_rows, go_up, go_down, t_r0, t_f1, t_r1, t_d, t_r2, t_f2, t_f3, t_n, t_mask, by_one, onehot, prefix, ones
 ):
     gx = lax.axis_index("gx")
     gy = lax.axis_index("gy")
+
+    go_up[...] = last_rows[...]
+    go_down[...] = first_rows[...]
 
     extent = [params[d] for d in range(4)]
     edge = [params[d] + params[4 + d] for d in range(4)]
@@ -151,7 +154,7 @@
     zero = jnp.zeros((ALL, LANES), F32)
     for t in range(4):
         for u, ks in (
-            (u0, (0, 12, 13, 14, 15, 16, 17)), (u1, (0, 13, 14, 15, 16, 17)), (u2, (0, 17)), (u3, (0, 17))
+            (u0, (0, 12, 13, 14, 15, 16, 17)), (u1, (0, 13, 14, 15, 16, 17)), (u2, (0, 15, 16, 17)), (u3, (0, 15, 16, 17))
         ):
             for k in ks:
                 u[t, k] = zero
@@ -250,7 +253,9 @@
             return 0
 
         shift(q, src, 0, even)
-        lax.fori_loop(0, 3 if q == 0 else 4, body, 0)
+        lax.fori_loop(0, 4 if last else 3, body, 0)
+        if q in (1, 2):
+            update(12, even)
 
     stage(0, u0, u1)
     stage(1, u1, u2)
@@ -275,18 +280,16 @@
     vmem = pltpu.VMEM
     field = probability[0]
     inner = field[:OLD0]
-    row_low = ring(inner[:, ROWS - FACE:], "gx", 1)
-    row_high = ring(inner[:, :FACE], "gx", -1)
     plane_low = ring(inner[:, :, LANES:], "gy", 1)
     plane_high = ring(inner[:, :, :LANES], "gy", -1)
-    corner = jnp.concatenate([row_high[:, :4], row_low[:, 4:]], axis=1)
-    corner_low = ring(corner[:, :, LANES:], "gy", 1)
-    corner_high = ring(corner[:, :, :LANES], "gy", -1)
     params = jnp.concatenate(
         [extent.astype(F32), slab_width.astype(F32), rate_const, hill_const, stoichiometry.T.reshape(32).astype(F32)]
     )
     whole = pl.BlockSpec(memory_space=pltpu.VMEM)
+    face = ((OLD0, FACE, PLANES * N4), F32)
     tables = [
+        face,
+        face,
         ((4, ALL, LANES), F32),
         ((4, ALL, LANES), F32),
         ((4, 4, ALL, LANES), F32),
@@ -299,20 +302,25 @@
         ((2 * LANES, 2 * LANES), BF16),
         ((DEVICES * SLOTS, N0 * ROWS), BF16),
     ]
-    made = pl.pallas_call(
+    go_up, go_down, *made = pl.pallas_call(
         prepare_tables,
         out_shape=[jax.ShapeDtypeStruct(*table) for table in tables],
-        in_specs=[pl.BlockSpec(memory_space=pltpu.SMEM), whole],
+        in_specs=[pl.BlockSpec(memory_space=pltpu.SMEM)] + [whole] * 3,
         out_specs=[whole] * len(tables),
         scratch_shapes=[vmem((128, 128), BF16), vmem((128, 128), BF16)],
         compiler_params=pltpu.CompilerParams(vmem_limit_bytes=12 * 1024 * 1024),
         cost_estimate=pl.CostEstimate(flops=10_000_000, bytes_accessed=16_000_000, transcendentals=0),
         name="prepare_tables",
-    )(params, new_owner.reshape(1, N0 * ROWS))
+    )(params, new_owner.reshape(1, N0 * ROWS), inner[:, ROWS - FACE:], inner[:, :FACE])
+    row_low = ring(go_up, "gx", 1)
+    row_high = ring(go_down, "gx", -1)
+    corner = jnp.concatenate([row_high[:, :4], row_low[:, 4:]], axis=1)
+    corner_low = ring(corner[:, :, LANES:], "gy", 1)
+    corner_high = ring(corner[:, :, :LANES], "gy", -1)
     sent = pl.pallas_call(
         advance,
         out_shape=jax.ShapeDtypeStruct((DEVICES * SLOTS, PLANES * N4), F32),
-        in_specs=[whole] * (7 + len(tables)),
+        in_specs=[whole] * (7 + len(made)),
         out_specs=whole,
         scratch_shapes=[
             vmem((4, N0 + 2, ALL, LANES), F32),

time: 78.2 us -> 76.1 us (0.973)
  blocking collectives: 38.6 us -> 33.4 us
  waiting for transfers between devices: 6.91 us -> 10.1 us
  Pallas kernels: 13.9 us -> 13 us
  starting transfers between devices: 15.6 us -> 16.5 us
    all_to_all x1, blocking collectives: 38.6 us -> 33.4 us  [shards(): lax.all_to_all(sent.reshape(DEVICES, SLOTS, PLANES * N4), ('gx', 'gy'), s...]
    ppermute x6, waiting for transfers between devices: 6.91 us -> 10.1 us  [ring(): lax.ppermute(values, axis, [(i, (i + shift) % count) for i in range(count)])]
    pallas_call x1, Pallas kernels: 11.6 us -> 10.7 us  [shards(): pl.pallas_call(advance, out_shape=jax.ShapeDtypeStruct((DEVICES * SLOTS,...]
    ppermute x6, starting transfers between devices: 15.6 us -> 16.5 us  [ring(): lax.ppermute(values, axis, [(i, (i + shift) % count) for i in range(count)])]
  transfers between devices with their start and end apart: 6 -> 6, of which waited for: 2 -> 3; matrix products, arithmetic and copies ran while one was open for 0% -> 0% of each run, Pallas kernels for 3% -> 3%
where the time goes in v3:
time: 76.1 us; the launch traced here: 76 us
  blocking collectives  33.4 us (44%)
  starting transfers between devices  16.5 us (22%)
  Pallas kernels  13 us (17%)
  waiting for transfers between devices  10.1 us (13%)
  local copies, waits for them, and re-layouts  2.86 us (4%)
    all_to_all x1, blocking collectives, shards(): lax.all_to_all(sent.reshape(DEVICES, SLOTS, PLANES * N4), ('gx', 'gy'), s...  33.4 us
    ppermute x6, starting transfers between devices, ring(): lax.ppermute(values, axis, [(i, (i + shift) % count) for i in range(count)])  16.5 us
    pallas_call x1, Pallas kernels, shards(): pl.pallas_call(advance, out_shape=jax.ShapeDtypeStruct((DEVICES * SLOTS,...  10.7 us
    ppermute x6, waiting for transfers between devices, ring(): lax.ppermute(values, axis, [(i, (i + shift) % count) for i in range(count)])  10.1 us
    pallas_call x1, Pallas kernels, shards(): pl.pallas_call(prepare_tables, out_shape=[jax.ShapeDtypeStruct(*table) fo...  2.27 us
  transfers between devices with their start and end apart: 6, of which 3 were waited for; matrix products, arithmetic and copies ran while one was open for 0% of the time, Pallas kernels for 3%

profile of v3, /device:TPU:0, one launch (start us, length us, event | category | flops | bytes accessed | tf_op | source)
XLA Modules:
  0.0 76.0 jit_solution(13947995444175302770)
XLA Ops:
  0.0 0.0 copy-start.3
  0.0 0.0 copy-start.1
  0.0 1.2 %slice_bitcast_fusion = f32[11,64,256]{2,1,0:T(8,128)S(1)} fusion(f32[1,16,64,256]{3,2,1,0:T(8,128)} %param.7), kind=kLoop, calls=%fused_computation | loop fusion | bytes 1441792 | tf_op jit(solution)/shard_map/slice | solution.py:282
  1.3 0.1 fusion.1
  1.4 6.2 %collective-permute-start.3 = (f32[11,64,128]{2,1,0:T(8,128)S(1)}, f32[11,64,128]{2,1,0:T(8,128)S(1)}, u32[]{:S(2)}, u32[]{:S(2)}) collective-permute-start(f32[11,64,128]{2,1,0:T(8,128)S(1)} %get-tuple-element.31), channel_id=1, source_target_pairs={{0,7},{1,0},{2,1},{3,2},{4,3},{5,4},{6,5},{7,6},{8,15},{9,8},{10,9... | collective-permute-start | bytes 1081352 | tf_op jit(solution)/shard_map/ppermute | solution.py:276
  7.6 0.0 collective-permute-start.2
  7.6 0.0 copy-done.2
  7.7 0.1 convert_element_type.19
  7.8 0.0 copy-done.4
  7.8 0.1 concatenate.6.params
  7.9 2.3 %prepare_tables.1 = (f32[11,8,256]{2,1,0:T(8,128)S(1)}, f32[11,8,256]{2,1,0:T(8,128)S(1)}, f32[4,88,128]{2,1,0:T(8,128)S(1)}, f32[4,88,128]{2,1,0:T(8,128)S(1)},...) custom-call(f32[56]{0:T(128)S(1)} %concatenate.6.params, ...), custom_call_target="tpu_custom_call" | custom-call | flops 10000000 | bytes 16000000 | tf_op jit(solution)/shard_map/prepare_tables/pallas_call | solution.py:305
  10.1 0.1 collective-permute-start
  10.2 3.8 %collective-permute-start.1 = (f32[11,8,256]{2,1,0:T(8,128)S(1)}, f32[11,8,256]{2,1,0:T(8,128)S(1)}, u32[]{:S(2)}, u32[]{:S(2)}) collective-permute-start(f32[11,8,256]{2,1,0:T(8,128)S(1)} %get-tuple-element.19), channel_id=1, source_target_pairs={{0,120},{8,0},{16,8},{24,16},{32,24},{40,32},{48,40},{56,48},{64,5... | collective-permute-start | bytes 270344 | tf_op jit(solution)/shard_map/ppermute | solution.py:276
  14.1 2.5 %collective-permute-done.row_low = f32[11,8,256]{2,1,0:T(8,128)S(1)} collective-permute-done((f32[11,8,256]{2,1,0:T(8,128)S(1)}, f32[11,8,256]{2,1,0:T(8,128)S(1)}, u32[]{:S(2)}, u32[]{:S(2)}) %collective-permute-start) | collective-permute-done | bytes 90144 | tf_op jit(solution)/shard_map/ppermute | solution.py:276
  16.5 0.0 collective-permute-done.1.row_high
  16.6 6.4 %collective-permute-start.5 = (f32[11,8,128]{2,1,0:T(8,128)S(1)}, f32[11,8,128]{2,1,0:T(8,128)S(1)}, u32[]{:S(2)}, u32[]{:S(2)}) collective-permute-start(f32[11,8,128]{2,1,0:T(8,128)S(1)} %get-tuple-element.35), channel_id=1, source_target_pairs={{0,7},{1,0},{2,1},{3,2},{4,3},{5,4},{6,5},{7,6},{8,15},{9,8},{10,9... | collective-permute-start | bytes 135176 | tf_op jit(solution)/shard_map/ppermute | solution.py:276
  23.0 0.0 collective-permute-start.4
  23.0 1.7 %collective-permute-done.5.corner_high = f32[11,8,128]{2,1,0:T(8,128)S(1)} collective-permute-done((f32[11,8,128]{2,1,0:T(8,128)S(1)}, f32[11,8,128]{2,1,0:T(8,128)S(1)}, u32[]{:S(2)}, u32[]{:S(2)}) %collective-permute-start.5) | collective-permute-done | bytes 45088 | tf_op jit(solution)/shard_map/ppermute | solution.py:276
  24.7 5.9 %collective-permute-done.4.corner_low = f32[11,8,128]{2,1,0:T(8,128)S(1)} collective-permute-done((f32[11,8,128]{2,1,0:T(8,128)S(1)}, f32[11,8,128]{2,1,0:T(8,128)S(1)}, u32[]{:S(2)}, u32[]{:S(2)}) %collective-permute-start.4) | collective-permute-done | bytes 45088 | tf_op jit(solution)/shard_map/ppermute | solution.py:276
  30.6 0.0 collective-permute-done.3.plane_high
  30.6 0.0 collective-permute-done.2.plane_low
  30.6 10.7 %advance.1 = f32[2048,256]{1,0:T(8,128)S(1)} custom-call(f32[16,64,256]{2,1,0:T(8,128)S(1)} %bitcast.9, f32[11,8,256]{2,1,0:T(8,128)S(1)} %collective-permute-done.row_low, f32[11,8,256]{2,1,0:T(8,128)S(1)} %collective-permute-done.1.row_high, f32[11,64,128]{2,1,0:T(8,128)S(1)} %collective-permute-done.2.plane_low, ...), custom_call_target="tpu_custom_call" | custom-call | tf_op jit(solution)/shard_map/advance/pallas_call | solution.py:320
  41.3 33.4 %all_to_all.5 = f32[128,16,256]{2,1,0:T(8,128)S(1)} all-to-all(f32[128,16,256]{2,1,0:T(8,128)S(1)} %bitcast.8), channel_id=1, replica_groups=mesh['gx'=16,'gy'=8] {'gx','gy'}, dimensions={0} | all-to-all | bytes 4194304 | tf_op jit(solution)/shard_map/all_to_all | solution.py:337
  74.7 1.3 %copy.9 = f32[1,128,16,256]{3,2,1,0:T(8,128)} copy(f32[1,128,16,256]{3,2,1,0:T(8,128)S(1)} %bitcast.11) | data formatting | bytes 4194304
  (17 shorter events, 0.1 us)
Async XLA Ops:
  0.0 30.6 %copy-start = (f32[1,16,64,256]{3,2,1,0:T(8,128)S(1)}, f32[1,16,64,256]{3,2,1,0:T(8,128)}, u32[]{:S(2)}) copy-start(f32[1,16,64,256]{3,2,1,0:T(8,128)} %param.7) | copy-start | bytes 3145732
  0.0 7.6 %copy-start.2 = (s32[8,4]{0,1:T(4,128)S(1)}, s32[8,4]{0,1:T(4,128)}, u32[]{:S(2)}) copy-start(s32[8,4]{0,1:T(4,128)} %param.12) | copy-start | bytes 388
  0.0 7.6 %copy-start.5 = (s32[4]{0:T(128)S(1)}, s32[4]{0:T(128)}, u32[]{:S(2)}) copy-start(s32[4]{0:T(128)} %param.8) | copy-start | bytes 52
  0.0 7.7 %copy-start.6 = (s32[4]{0:T(128)S(1)}, s32[4]{0:T(128)}, u32[]{:S(2)}) copy-start(s32[4]{0:T(128)} %param.9) | copy-start | bytes 52
  0.0 7.8 %copy-start.4 = (f32[8]{0:T(128)S(1)}, f32[8]{0:T(128)}, u32[]{:S(2)}) copy-start(f32[8]{0:T(128)} %param.11) | copy-start | bytes 100
  0.0 7.8 %copy-start.3 = (f32[8]{0:T(128)S(1)}, f32[8]{0:T(128)}, u32[]{:S(2)}) copy-start(f32[8]{0:T(128)} %param.10) | copy-start | bytes 100
  0.0 7.8 %copy-start.1 = (s32[1,1,1024,1]{2,3,1,0:T(1,128)S(1)}, s32[1,1,1024,1]{2,3,1,0:T(1,128)}, u32[]{:S(2)}) copy-start(s32[1,1,1024,1]{2,3,1,0:T(1,128)} %param.13) | copy-start | bytes 12292
  1.4 29.3 %collective-permute-start.3 = (f32[11,64,128]{2,1,0:T(8,128)S(1)}, f32[11,64,128]{2,1,0:T(8,128)S(1)}, u32[]{:S(2)}, u32[]{:S(2)}) collective-permute-start(f32[11,64,128]{2,1,0:T(8,128)S(1)} %get-tuple-element.31), channel_id=1, source_target_pairs={{0,7},{1,0},{2,1},{3,2},{4,3},{5,4},{6,5},{7,6},{8,15},{9,8},{10,9... | collective-permute-start | bytes 1081352 | tf_op jit(solution)/shard_map/ppermute | solution.py:276
  7.6 23.0 %collective-permute-start.2 = (f32[11,64,128]{2,1,0:T(8,128)S(1)}, f32[11,64,128]{2,1,0:T(8,128)S(1)}, u32[]{:S(2)}, u32[]{:S(2)}) collective-permute-start(f32[11,64,128]{2,1,0:T(8,128)S(1)} %get-tuple-element.32), channel_id=1, source_target_pairs={{0,1},{1,2},{2,3},{3,4},{4,5},{5,6},{6,7},{7,0},{8,9},{9,10},{10,1... | collective-permute-start | bytes 1081352 | tf_op jit(solution)/shard_map/ppermute | solution.py:276
  10.1 6.4 %collective-permute-start = (f32[11,8,256]{2,1,0:T(8,128)S(1)}, f32[11,8,256]{2,1,0:T(8,128)S(1)}, u32[]{:S(2)}, u32[]{:S(2)}) collective-permute-start(f32[11,8,256]{2,1,0:T(8,128)S(1)} %get-tuple-element.18), channel_id=1, source_target_pairs={{0,8},{8,16},{16,24},{24,32},{32,40},{40,48},{48,56},{56,64},{64,7... | collective-permute-start | bytes 270344 | tf_op jit(solution)/shard_map/ppermute | solution.py:276
  10.2 6.3 %collective-permute-start.1 = (f32[11,8,256]{2,1,0:T(8,128)S(1)}, f32[11,8,256]{2,1,0:T(8,128)S(1)}, u32[]{:S(2)}, u32[]{:S(2)}) collective-permute-start(f32[11,8,256]{2,1,0:T(8,128)S(1)} %get-tuple-element.19), channel_id=1, source_target_pairs={{0,120},{8,0},{16,8},{24,16},{32,24},{40,32},{48,40},{56,48},{64,5... | collective-permute-start | bytes 270344 | tf_op jit(solution)/shard_map/ppermute | solution.py:276
  16.6 8.1 %collective-permute-start.5 = (f32[11,8,128]{2,1,0:T(8,128)S(1)}, f32[11,8,128]{2,1,0:T(8,128)S(1)}, u32[]{:S(2)}, u32[]{:S(2)}) collective-permute-start(f32[11,8,128]{2,1,0:T(8,128)S(1)} %get-tuple-element.35), channel_id=1, source_target_pairs={{0,7},{1,0},{2,1},{3,2},{4,3},{5,4},{6,5},{7,6},{8,15},{9,8},{10,9... | collective-permute-start | bytes 135176 | tf_op jit(solution)/shard_map/ppermute | solution.py:276
  23.0 7.7 %collective-permute-start.4 = (f32[11,8,128]{2,1,0:T(8,128)S(1)}, f32[11,8,128]{2,1,0:T(8,128)S(1)}, u32[]{:S(2)}, u32[]{:S(2)}) collective-permute-start(f32[11,8,128]{2,1,0:T(8,128)S(1)} %get-tuple-element.36), channel_id=1, source_target_pairs={{0,1},{1,2},{2,3},{3,4},{4,5},{5,6},{6,7},{7,0},{8,9},{9,10},{10,1... | collective-permute-start | bytes 135176 | tf_op jit(solution)/shard_map/ppermute | solution.py:276

commit v4 on v3

--- a/solution.py
+++ b/solution.py
@@ -158,6 +158,8 @@
         ):
             for k in ks:
                 u[t, k] = zero
+    row8 = lax.broadcasted_iota(jnp.int32, (8, LANES), 0)
+
     def prepare(n0, _):
         def put(t, row, count, values):
             rows = pl.ds(row, count)
@@ -169,12 +171,20 @@
             put(1 + h, OWN + ROWS, REACH, row_high[n0, pl.ds(0, REACH), lanes])
             put(1 + h, OWN, ROWS, prob[n0, :, lanes])
         for t, plane, corner in ((0, plane_low, corner_low), (3, plane_high, corner_high)):
-            put(t, FIRST, REACH, corner[n0, pl.ds(REACH, REACH), :])
-            put(t, OWN + ROWS, REACH, corner[n0, pl.ds(0, REACH), :])
+            wide = [jnp.broadcast_to(corner[n0, pl.ds(j, 1), :], (8, LANES)) for j in range(3)]
+            turned = LANES - N4 if t == 0 else N4
+            block = jnp.where(row8 == 3, wide[0], jnp.zeros((8, LANES), F32))
+            block = jnp.where(row8 == 2, wide[1], block)
+            block = jnp.where(row8 == 1, pltpu.roll(wide[0], turned, 1), block)
+            block = jnp.where(row8 == 4, wide[2], block)
+            block = jnp.where(row8 == 5, pltpu.roll(wide[1], 2 * N4, 1), block)
+            block = jnp.where(row8 == 6, pltpu.roll(wide[2], turned, 1), block)
+            put(t, FIRST, REACH, block[:REACH])
+            put(t, OWN + ROWS, REACH, block[REACH:])
             put(t, OWN, ROWS, plane[n0])
         return 0
 
-    lax.fori_loop(0, OLD0, prepare, 0)
+    lax.fori_loop(0, OLD0, prepare, 0, unroll=True)
 
     lane = lax.broadcasted_iota(jnp.int32, (8, LANES), 1)
     first_plane = lane < N4
@@ -271,6 +281,20 @@
     lax.fori_loop(0, DEVICES * SLOTS // BLOCK, permute, 0)
 
 
+def pack_corners(row_low, row_high, to_above, to_below):
+    lane = lax.broadcasted_iota(jnp.int32, (1, LANES), 1)
+    for n0 in range(OLD0):
+        for out, start, one in ((to_above, LANES, N4), (to_below, 0, LANES - N4)):
+            low = row_low[n0, :, pl.ds(start, LANES)]
+            high = row_high[n0, :, pl.ds(start, LANES)]
+            up = start > 0
+            far_one = lane < N4 if up else lane >= LANES - N4
+            far_two = lane < 2 * N4 if up else lane >= 2 * N4
+            out[n0, pl.ds(0, 1), :] = jnp.where(far_one, pltpu.roll(low, one, 1)[5:6], low[7:8])
+            out[n0, pl.ds(1, 1), :] = jnp.where(far_two, pltpu.roll(high, 2 * N4, 1)[1:2], low[6:7])
+            out[n0, pl.ds(2, 1), :] = jnp.where(far_one, pltpu.roll(high, one, 1)[2:3], high[0:1])
+
+
 def ring(values, axis, shift):
     count = lax.axis_size(axis)
     return lax.ppermute(values, axis, [(i, (i + shift) % count) for i in range(count)])
@@ -314,9 +338,17 @@
     )(params, new_owner.reshape(1, N0 * ROWS), inner[:, ROWS - FACE:], inner[:, :FACE])
     row_low = ring(go_up, "gx", 1)
     row_high = ring(go_down, "gx", -1)
-    corner = jnp.concatenate([row_high[:, :4], row_low[:, 4:]], axis=1)
-    corner_low = ring(corner[:, :, LANES:], "gy", 1)
-    corner_high = ring(corner[:, :, :LANES], "gy", -1)
+    corner = jax.ShapeDtypeStruct((OLD0, 3, LANES), F32)
+    to_above, to_below = pl.pallas_call(
+        pack_corners,
+        out_shape=[corner, corner],
+        in_specs=[whole, whole],
+        out_specs=[whole, whole],
+        compiler_params=pltpu.CompilerParams(vmem_limit_bytes=4 * 1024 * 1024),
+        name="pack_corners",
+    )(row_low, row_high)
+    corner_low = ring(to_above, "gy", 1)
+    corner_high = ring(to_below, "gy", -1)
     sent = pl.pallas_call(
         advance,
         out_shape=jax.ShapeDtypeStruct((DEVICES * SLOTS, PLANES * N4), F32),

time: 76.1 us -> 75.3 us (0.989)
  waiting for transfers between devices: 10.1 us -> 4.4 us
  blocking collectives: 33.4 us -> 38.1 us
    ppermute x6, waiting for transfers between devices: 10.1 us -> 4.4 us  [ring(): lax.ppermute(values, axis, [(i, (i + shift) % count) for i in range(count)])]
    all_to_all x1, blocking collectives: 33.4 us -> 38.1 us  [shards(): lax.all_to_all(sent.reshape(DEVICES, SLOTS, PLANES * N4), ('gx', 'gy'), s...]
where the time goes in v4:
time: 75.3 us; the launch traced here: 75.1 us
  blocking collectives  38.1 us (51%)
  starting transfers between devices  16.6 us (22%)
  Pallas kernels  13 us (17%)
  waiting for transfers between devices  4.4 us (6%)
  local copies, waits for them, and re-layouts  2.85 us (4%)
    all_to_all x1, blocking collectives, shards(): lax.all_to_all(sent.reshape(DEVICES, SLOTS, PLANES * N4), ('gx', 'gy'), s...  38.1 us
    ppermute x6, starting transfers between devices, ring(): lax.ppermute(values, axis, [(i, (i + shift) % count) for i in range(count)])  16.6 us
    pallas_call x1, Pallas kernels, shards(): pl.pallas_call(advance, out_shape=jax.ShapeDtypeStruct((DEVICES * SLOTS,...  10.5 us
    ppermute x6, waiting for transfers between devices, ring(): lax.ppermute(values, axis, [(i, (i + shift) % count) for i in range(count)])  4.4 us
    pallas_call x1, Pallas kernels, shards(): pl.pallas_call(prepare_tables, out_shape=[jax.ShapeDtypeStruct(*table) fo...  2.28 us
  transfers between devices with their start and end apart: 6, of which 3 were waited for; matrix products, arithmetic and copies ran while one was open for 0% of the time, Pallas kernels for 3%

profile of v4, /device:TPU:0, one launch (start us, length us, event | category | flops | bytes accessed | tf_op | source)
XLA Modules:
  0.0 75.1 jit_solution(10588882882785982052)
XLA Ops:
  0.0 0.0 copy-start.3
  0.0 0.0 copy-start.1
  0.0 1.3 %slice_bitcast_fusion = f32[11,64,256]{2,1,0:T(8,128)S(1)} fusion(f32[1,16,64,256]{3,2,1,0:T(8,128)} %param.7), kind=kLoop, calls=%fused_computation | loop fusion | bytes 1441792 | tf_op jit(solution)/shard_map/slice | solution.py:306
  1.3 0.1 fusion
  1.4 6.2 %collective-permute-start.3 = (f32[11,64,128]{2,1,0:T(8,128)S(1)}, f32[11,64,128]{2,1,0:T(8,128)S(1)}, u32[]{:S(2)}, u32[]{:S(2)}) collective-permute-start(f32[11,64,128]{2,1,0:T(8,128)S(1)} %get-tuple-element.35), channel_id=1, source_target_pairs={{0,7},{1,0},{2,1},{3,2},{4,3},{5,4},{6,5},{7,6},{8,15},{9,8},{10,9... | collective-permute-start | bytes 1081352 | tf_op jit(solution)/shard_map/ppermute | solution.py:300
  7.6 0.0 collective-permute-start.2
  7.6 0.0 copy-done.2
  7.7 0.1 convert_element_type.19
  7.8 0.1 concatenate.3.params
  7.9 2.3 %prepare_tables.1 = (f32[11,8,256]{2,1,0:T(8,128)S(1)}, f32[11,8,256]{2,1,0:T(8,128)S(1)}, f32[4,88,128]{2,1,0:T(8,128)S(1)}, f32[4,88,128]{2,1,0:T(8,128)S(1)},...) custom-call(f32[56]{0:T(128)S(1)} %concatenate.3.params, ...), custom_call_target="tpu_custom_call" | custom-call | flops 10000000 | bytes 16000000 | tf_op jit(solution)/shard_map/prepare_tables/pallas_call | solution.py:329
  10.2 0.1 collective-permute-start
  10.2 3.8 %collective-permute-start.1 = (f32[11,8,256]{2,1,0:T(8,128)S(1)}, f32[11,8,256]{2,1,0:T(8,128)S(1)}, u32[]{:S(2)}, u32[]{:S(2)}) collective-permute-start(f32[11,8,256]{2,1,0:T(8,128)S(1)} %get-tuple-element.21), channel_id=1, source_target_pairs={{0,120},{8,0},{16,8},{24,16},{32,24},{40,32},{48,40},{56,48},{64,5... | collective-permute-start | bytes 270344 | tf_op jit(solution)/shard_map/ppermute | solution.py:300
  14.1 2.4 %collective-permute-done.row_low = f32[11,8,256]{2,1,0:T(8,128)S(1)} collective-permute-done((f32[11,8,256]{2,1,0:T(8,128)S(1)}, f32[11,8,256]{2,1,0:T(8,128)S(1)}, u32[]{:S(2)}, u32[]{:S(2)}) %collective-permute-start) | collective-permute-done | bytes 90144 | tf_op jit(solution)/shard_map/ppermute | solution.py:300
  16.5 0.0 collective-permute-done.1.row_high
  16.5 0.1 pack_corners.1
  16.7 3.1 %collective-permute-start.4 = (f32[11,3,128]{2,1,0:T(4,128)S(1)}, f32[11,3,128]{2,1,0:T(4,128)S(1)}, u32[]{:S(2)}, u32[]{:S(2)}) collective-permute-start(f32[11,3,128]{2,1,0:T(4,128)S(1)} %get-tuple-element.22), channel_id=1, source_target_pairs={{0,1},{1,2},{2,3},{3,4},{4,5},{5,6},{6,7},{7,0},{8,9},{9,10},{10,1... | collective-permute-start | bytes 50696 | tf_op jit(solution)/shard_map/ppermute | solution.py:300
  19.7 3.4 %collective-permute-start.5 = (f32[11,3,128]{2,1,0:T(4,128)S(1)}, f32[11,3,128]{2,1,0:T(4,128)S(1)}, u32[]{:S(2)}, u32[]{:S(2)}) collective-permute-start(f32[11,3,128]{2,1,0:T(4,128)S(1)} %get-tuple-element.23), channel_id=1, source_target_pairs={{0,7},{1,0},{2,1},{3,2},{4,3},{5,4},{6,5},{7,6},{8,15},{9,8},{10,9... | collective-permute-start | bytes 50696 | tf_op jit(solution)/shard_map/ppermute | solution.py:300
  23.1 1.7 %collective-permute-done.4.corner_low = f32[11,3,128]{2,1,0:T(4,128)S(1)} collective-permute-done((f32[11,3,128]{2,1,0:T(4,128)S(1)}, f32[11,3,128]{2,1,0:T(4,128)S(1)}, u32[]{:S(2)}, u32[]{:S(2)}) %collective-permute-start.4) | collective-permute-done | bytes 16928 | tf_op jit(solution)/shard_map/ppermute | solution.py:300
  24.8 0.2 collective-permute-done.5.corner_high
  25.1 0.0 collective-permute-done.3.plane_high
  25.1 0.0 collective-permute-done.2.plane_low
  25.1 10.5 %advance.1 = f32[2048,256]{1,0:T(8,128)S(1)} custom-call(f32[16,64,256]{2,1,0:T(8,128)S(1)} %bitcast.9, f32[11,8,256]{2,1,0:T(8,128)S(1)} %collective-permute-done.row_low, f32[11,8,256]{2,1,0:T(8,128)S(1)} %collective-permute-done.1.row_high, f32[11,64,128]{2,1,0:T(8,128)S(1)} %collective-permute-done.2.plane_low, ...), custom_call_target="tpu_custom_call" | custom-call | tf_op jit(solution)/shard_map/advance/pallas_call | solution.py:352
  35.6 38.1 %all_to_all.5 = f32[128,16,256]{2,1,0:T(8,128)S(1)} all-to-all(f32[128,16,256]{2,1,0:T(8,128)S(1)} %bitcast.8), channel_id=1, replica_groups=mesh['gx'=16,'gy'=8] {'gx','gy'}, dimensions={0} | all-to-all | bytes 4194304 | tf_op jit(solution)/shard_map/all_to_all | solution.py:369
  73.8 1.3 %copy.9 = f32[1,128,16,256]{3,2,1,0:T(8,128)} copy(f32[1,128,16,256]{3,2,1,0:T(8,128)S(1)} %bitcast.11) | data formatting | bytes 4194304
  (15 shorter events, 0.0 us)
Async XLA Ops:
  0.0 25.1 %copy-start = (f32[1,16,64,256]{3,2,1,0:T(8,128)S(1)}, f32[1,16,64,256]{3,2,1,0:T(8,128)}, u32[]{:S(2)}) copy-start(f32[1,16,64,256]{3,2,1,0:T(8,128)} %param.7) | copy-start | bytes 3145732
  0.0 7.6 %copy-start.2 = (s32[8,4]{0,1:T(4,128)S(1)}, s32[8,4]{0,1:T(4,128)}, u32[]{:S(2)}) copy-start(s32[8,4]{0,1:T(4,128)} %param.12) | copy-start | bytes 388
  0.0 7.6 %copy-start.5 = (s32[4]{0:T(128)S(1)}, s32[4]{0:T(128)}, u32[]{:S(2)}) copy-start(s32[4]{0:T(128)} %param.8) | copy-start | bytes 52
  0.0 7.6 %copy-start.6 = (s32[4]{0:T(128)S(1)}, s32[4]{0:T(128)}, u32[]{:S(2)}) copy-start(s32[4]{0:T(128)} %param.9) | copy-start | bytes 52
  0.0 7.7 %copy-start.4 = (f32[8]{0:T(128)S(1)}, f32[8]{0:T(128)}, u32[]{:S(2)}) copy-start(f32[8]{0:T(128)} %param.11) | copy-start | bytes 100
  0.0 7.7 %copy-start.3 = (f32[8]{0:T(128)S(1)}, f32[8]{0:T(128)}, u32[]{:S(2)}) copy-start(f32[8]{0:T(128)} %param.10) | copy-start | bytes 100
  0.0 7.8 %copy-start.1 = (s32[1,1,1024,1]{2,3,1,0:T(1,128)S(1)}, s32[1,1,1024,1]{2,3,1,0:T(1,128)}, u32[]{:S(2)}) copy-start(s32[1,1,1024,1]{2,3,1,0:T(1,128)} %param.13) | copy-start | bytes 12292
  1.4 23.7 %collective-permute-start.3 = (f32[11,64,128]{2,1,0:T(8,128)S(1)}, f32[11,64,128]{2,1,0:T(8,128)S(1)}, u32[]{:S(2)}, u32[]{:S(2)}) collective-permute-start(f32[11,64,128]{2,1,0:T(8,128)S(1)} %get-tuple-element.35), channel_id=1, source_target_pairs={{0,7},{1,0},{2,1},{3,2},{4,3},{5,4},{6,5},{7,6},{8,15},{9,8},{10,9... | collective-permute-start | bytes 1081352 | tf_op jit(solution)/shard_map/ppermute | solution.py:300
  7.6 17.5 %collective-permute-start.2 = (f32[11,64,128]{2,1,0:T(8,128)S(1)}, f32[11,64,128]{2,1,0:T(8,128)S(1)}, u32[]{:S(2)}, u32[]{:S(2)}) collective-permute-start(f32[11,64,128]{2,1,0:T(8,128)S(1)} %get-tuple-element.36), channel_id=1, source_target_pairs={{0,1},{1,2},{2,3},{3,4},{4,5},{5,6},{6,7},{7,0},{8,9},{9,10},{10,1... | collective-permute-start | bytes 1081352 | tf_op jit(solution)/shard_map/ppermute | solution.py:300
  10.2 6.4 %collective-permute-start = (f32[11,8,256]{2,1,0:T(8,128)S(1)}, f32[11,8,256]{2,1,0:T(8,128)S(1)}, u32[]{:S(2)}, u32[]{:S(2)}) collective-permute-start(f32[11,8,256]{2,1,0:T(8,128)S(1)} %get-tuple-element.20), channel_id=1, source_target_pairs={{0,8},{8,16},{16,24},{24,32},{32,40},{40,48},{48,56},{56,64},{64,7... | collective-permute-start | bytes 270344 | tf_op jit(solution)/shard_map/ppermute | solution.py:300
  10.2 6.3 %collective-permute-start.1 = (f32[11,8,256]{2,1,0:T(8,128)S(1)}, f32[11,8,256]{2,1,0:T(8,128)S(1)}, u32[]{:S(2)}, u32[]{:S(2)}) collective-permute-start(f32[11,8,256]{2,1,0:T(8,128)S(1)} %get-tuple-element.21), channel_id=1, source_target_pairs={{0,120},{8,0},{16,8},{24,16},{32,24},{40,32},{48,40},{56,48},{64,5... | collective-permute-start | bytes 270344 | tf_op jit(solution)/shard_map/ppermute | solution.py:300
  16.7 8.2 %collective-permute-start.4 = (f32[11,3,128]{2,1,0:T(4,128)S(1)}, f32[11,3,128]{2,1,0:T(4,128)S(1)}, u32[]{:S(2)}, u32[]{:S(2)}) collective-permute-start(f32[11,3,128]{2,1,0:T(4,128)S(1)} %get-tuple-element.22), channel_id=1, source_target_pairs={{0,1},{1,2},{2,3},{3,4},{4,5},{5,6},{6,7},{7,0},{8,9},{9,10},{10,1... | collective-permute-start | bytes 50696 | tf_op jit(solution)/shard_map/ppermute | solution.py:300
  19.7 5.3 %collective-permute-start.5 = (f32[11,3,128]{2,1,0:T(4,128)S(1)}, f32[11,3,128]{2,1,0:T(4,128)S(1)}, u32[]{:S(2)}, u32[]{:S(2)}) collective-permute-start(f32[11,3,128]{2,1,0:T(4,128)S(1)} %get-tuple-element.23), channel_id=1, source_target_pairs={{0,7},{1,0},{2,1},{3,2},{4,3},{5,4},{6,5},{7,6},{8,15},{9,8},{10,9... | collective-permute-start | bytes 50696 | tf_op jit(solution)/shard_map/ppermute | solution.py:300

commit v5 on v4

--- a/solution.py
+++ b/solution.py
@@ -25,7 +25,7 @@
 GROUPS = 9
 WORK = 8 * GROUPS
 ALL = WORK + 2 * FIRST
-BLOCK = 512
+BLOCK = 1024
 
 
 def prepare_tables(
@@ -106,7 +106,7 @@
         for q in range(4):
             t_n[q, n0, 0] = steps[q] * (rise_3 * in_3)
             t_n[q, n0, 1] = steps[q] * fall_0
-            t_n[q, n0, 2] = (-steps[q]) * leave_0
+            t_n[q, n0, 2] = (1.0 if q == 0 else 0.0) - steps[q] * leave_0
             t_n[q, n0, 3] = in_0
         return 0
 
@@ -231,7 +231,9 @@
                         c = centre[k][a]
                         from_below = jnp.where(first_plane, up[k][a - 1], up[k][a]) if a > 0 else up[k][a]
                         from_above = jnp.where(last_plane, down[k][a + 1], down[k][a]) if a < 3 else down[k][a]
-                        acc = u0[a, n0 + k + 1, rows, :] + (d + l0[k]) * c
+                        acc = (d + l0[k]) * c
+                        if q > 0:
+                            acc = u0[a, n0 + k + 1, rows, :] + acc
                         acc = acc + (r0[k] * before[k] + f0[k] * after[k])
                         acc = acc + (
                             r1 * src[a, n0 + k + 1, pl.ds(row - 1, 8), :]

time: 75.3 us -> 74.9 us (level)
  no operation moved by 1% of the time
where the time goes in v5:
time: 74.9 us; the launch traced here: 74.7 us
  blocking collectives  38.2 us (51%)
  starting transfers between devices  16.6 us (22%)
  Pallas kernels  12.6 us (17%)
  waiting for transfers between devices  4.39 us (6%)
  local copies, waits for them, and re-layouts  2.85 us (4%)
    all_to_all x1, blocking collectives, shards(): lax.all_to_all(sent.reshape(DEVICES, SLOTS, PLANES * N4), ('gx', 'gy'), s...  38.2 us
    ppermute x6, starting transfers between devices, ring(): lax.ppermute(values, axis, [(i, (i + shift) % count) for i in range(count)])  16.6 us
    pallas_call x1, Pallas kernels, shards(): pl.pallas_call(advance, out_shape=jax.ShapeDtypeStruct((DEVICES * SLOTS,...  10.1 us
    ppermute x6, waiting for transfers between devices, ring(): lax.ppermute(values, axis, [(i, (i + shift) % count) for i in range(count)])  4.39 us
    pallas_call x1, Pallas kernels, shards(): pl.pallas_call(prepare_tables, out_shape=[jax.ShapeDtypeStruct(*table) fo...  2.29 us
  transfers between devices with their start and end apart: 6, of which 3 were waited for; matrix products, arithmetic and copies ran while one was open for 0% of the time, Pallas kernels for 3%

profile of v5, /device:TPU:0, one launch (start us, length us, event | category | flops | bytes accessed | tf_op | source)
XLA Modules:
  0.0 74.7 jit_solution(15445495495584673534)
XLA Ops:
  0.0 0.0 copy-start.3
  0.0 0.0 copy-start.1
  0.0 1.3 %slice_bitcast_fusion = f32[11,64,256]{2,1,0:T(8,128)S(1)} fusion(f32[1,16,64,256]{3,2,1,0:T(8,128)} %param.7), kind=kLoop, calls=%fused_computation | loop fusion | bytes 1441792 | tf_op jit(solution)/shard_map/slice | solution.py:308
  1.3 0.1 fusion
  1.4 6.2 %collective-permute-start.3 = (f32[11,64,128]{2,1,0:T(8,128)S(1)}, f32[11,64,128]{2,1,0:T(8,128)S(1)}, u32[]{:S(2)}, u32[]{:S(2)}) collective-permute-start(f32[11,64,128]{2,1,0:T(8,128)S(1)} %get-tuple-element.35), channel_id=1, source_target_pairs={{0,7},{1,0},{2,1},{3,2},{4,3},{5,4},{6,5},{7,6},{8,15},{9,8},{10,9... | collective-permute-start | bytes 1081352 | tf_op jit(solution)/shard_map/ppermute | solution.py:302
  7.6 0.0 collective-permute-start.2
  7.6 0.0 copy-done.6
  7.7 0.1 convert_element_type.19
  7.8 0.1 concatenate.3.params
  7.9 2.3 %prepare_tables.1 = (f32[11,8,256]{2,1,0:T(8,128)S(1)}, f32[11,8,256]{2,1,0:T(8,128)S(1)}, f32[4,88,128]{2,1,0:T(8,128)S(1)}, f32[4,88,128]{2,1,0:T(8,128)S(1)},...) custom-call(f32[56]{0:T(128)S(1)} %concatenate.3.params, ...), custom_call_target="tpu_custom_call" | custom-call | flops 10000000 | bytes 16000000 | tf_op jit(solution)/shard_map/prepare_tables/pallas_call | solution.py:331
  10.2 0.1 collective-permute-start
  10.2 3.8 %collective-permute-start.1 = (f32[11,8,256]{2,1,0:T(8,128)S(1)}, f32[11,8,256]{2,1,0:T(8,128)S(1)}, u32[]{:S(2)}, u32[]{:S(2)}) collective-permute-start(f32[11,8,256]{2,1,0:T(8,128)S(1)} %get-tuple-element.21), channel_id=1, source_target_pairs={{0,120},{8,0},{16,8},{24,16},{32,24},{40,32},{48,40},{56,48},{64,5... | collective-permute-start | bytes 270344 | tf_op jit(solution)/shard_map/ppermute | solution.py:302
  14.1 2.4 %collective-permute-done.row_low = f32[11,8,256]{2,1,0:T(8,128)S(1)} collective-permute-done((f32[11,8,256]{2,1,0:T(8,128)S(1)}, f32[11,8,256]{2,1,0:T(8,128)S(1)}, u32[]{:S(2)}, u32[]{:S(2)}) %collective-permute-start) | collective-permute-done | bytes 90144 | tf_op jit(solution)/shard_map/ppermute | solution.py:302
  16.5 0.0 collective-permute-done.1.row_high
  16.5 0.1 pack_corners.1
  16.7 3.1 %collective-permute-start.4 = (f32[11,3,128]{2,1,0:T(4,128)S(1)}, f32[11,3,128]{2,1,0:T(4,128)S(1)}, u32[]{:S(2)}, u32[]{:S(2)}) collective-permute-start(f32[11,3,128]{2,1,0:T(4,128)S(1)} %get-tuple-element.22), channel_id=1, source_target_pairs={{0,1},{1,2},{2,3},{3,4},{4,5},{5,6},{6,7},{7,0},{8,9},{9,10},{10,1... | collective-permute-start | bytes 50696 | tf_op jit(solution)/shard_map/ppermute | solution.py:302
  19.8 3.4 %collective-permute-start.5 = (f32[11,3,128]{2,1,0:T(4,128)S(1)}, f32[11,3,128]{2,1,0:T(4,128)S(1)}, u32[]{:S(2)}, u32[]{:S(2)}) collective-permute-start(f32[11,3,128]{2,1,0:T(4,128)S(1)} %get-tuple-element.23), channel_id=1, source_target_pairs={{0,7},{1,0},{2,1},{3,2},{4,3},{5,4},{6,5},{7,6},{8,15},{9,8},{10,9... | collective-permute-start | bytes 50696 | tf_op jit(solution)/shard_map/ppermute | solution.py:302
  23.1 1.7 %collective-permute-done.4.corner_low = f32[11,3,128]{2,1,0:T(4,128)S(1)} collective-permute-done((f32[11,3,128]{2,1,0:T(4,128)S(1)}, f32[11,3,128]{2,1,0:T(4,128)S(1)}, u32[]{:S(2)}, u32[]{:S(2)}) %collective-permute-start.4) | collective-permute-done | bytes 16928 | tf_op jit(solution)/shard_map/ppermute | solution.py:302
  24.8 0.2 collective-permute-done.5.corner_high
  25.1 0.0 collective-permute-done.3.plane_high
  25.1 0.0 collective-permute-done.2.plane_low
  25.1 10.1 %advance.1 = f32[2048,256]{1,0:T(8,128)S(1)} custom-call(f32[16,64,256]{2,1,0:T(8,128)S(1)} %bitcast.9, f32[11,8,256]{2,1,0:T(8,128)S(1)} %collective-permute-done.row_low, f32[11,8,256]{2,1,0:T(8,128)S(1)} %collective-permute-done.1.row_high, f32[11,64,128]{2,1,0:T(8,128)S(1)} %collective-permute-done.2.plane_low, ...), custom_call_target="tpu_custom_call" | custom-call | tf_op jit(solution)/shard_map/advance/pallas_call | solution.py:354
  35.2 38.2 %all_to_all.5 = f32[128,16,256]{2,1,0:T(8,128)S(1)} all-to-all(f32[128,16,256]{2,1,0:T(8,128)S(1)} %bitcast.8), channel_id=1, replica_groups=mesh['gx'=16,'gy'=8] {'gx','gy'}, dimensions={0} | all-to-all | bytes 4194304 | tf_op jit(solution)/shard_map/all_to_all | solution.py:371
  73.4 1.3 %copy.9 = f32[1,128,16,256]{3,2,1,0:T(8,128)} copy(f32[1,128,16,256]{3,2,1,0:T(8,128)S(1)} %bitcast.11) | data formatting | bytes 4194304
  (15 shorter events, 0.0 us)
Async XLA Ops:
  0.0 25.1 %copy-start = (f32[1,16,64,256]{3,2,1,0:T(8,128)S(1)}, f32[1,16,64,256]{3,2,1,0:T(8,128)}, u32[]{:S(2)}) copy-start(f32[1,16,64,256]{3,2,1,0:T(8,128)} %param.7) | copy-start | bytes 3145732
  0.0 7.6 %copy-start.2 = (s32[8,4]{0,1:T(4,128)S(1)}, s32[8,4]{0,1:T(4,128)}, u32[]{:S(2)}) copy-start(s32[8,4]{0,1:T(4,128)} %param.12) | copy-start | bytes 388
  0.0 7.6 %copy-start.5 = (s32[4]{0:T(128)S(1)}, s32[4]{0:T(128)}, u32[]{:S(2)}) copy-start(s32[4]{0:T(128)} %param.8) | copy-start | bytes 52
  0.0 7.6 %copy-start.6 = (s32[4]{0:T(128)S(1)}, s32[4]{0:T(128)}, u32[]{:S(2)}) copy-start(s32[4]{0:T(128)} %param.9) | copy-start | bytes 52
  0.0 7.7 %copy-start.4 = (f32[8]{0:T(128)S(1)}, f32[8]{0:T(128)}, u32[]{:S(2)}) copy-start(f32[8]{0:T(128)} %param.11) | copy-start | bytes 100
  0.0 7.7 %copy-start.3 = (f32[8]{0:T(128)S(1)}, f32[8]{0:T(128)}, u32[]{:S(2)}) copy-start(f32[8]{0:T(128)} %param.10) | copy-start | bytes 100
  0.0 7.8 %copy-start.1 = (s32[1,1,1024,1]{2,3,1,0:T(1,128)S(1)}, s32[1,1,1024,1]{2,3,1,0:T(1,128)}, u32[]{:S(2)}) copy-start(s32[1,1,1024,1]{2,3,1,0:T(1,128)} %param.13) | copy-start | bytes 12292
  1.4 23.7 %collective-permute-start.3 = (f32[11,64,128]{2,1,0:T(8,128)S(1)}, f32[11,64,128]{2,1,0:T(8,128)S(1)}, u32[]{:S(2)}, u32[]{:S(2)}) collective-permute-start(f32[11,64,128]{2,1,0:T(8,128)S(1)} %get-tuple-element.35), channel_id=1, source_target_pairs={{0,7},{1,0},{2,1},{3,2},{4,3},{5,4},{6,5},{7,6},{8,15},{9,8},{10,9... | collective-permute-start | bytes 1081352 | tf_op jit(solution)/shard_map/ppermute | solution.py:302
  7.6 17.5 %collective-permute-start.2 = (f32[11,64,128]{2,1,0:T(8,128)S(1)}, f32[11,64,128]{2,1,0:T(8,128)S(1)}, u32[]{:S(2)}, u32[]{:S(2)}) collective-permute-start(f32[11,64,128]{2,1,0:T(8,128)S(1)} %get-tuple-element.36), channel_id=1, source_target_pairs={{0,1},{1,2},{2,3},{3,4},{4,5},{5,6},{6,7},{7,0},{8,9},{9,10},{10,1... | collective-permute-start | bytes 1081352 | tf_op jit(solution)/shard_map/ppermute | solution.py:302
  10.2 6.4 %collective-permute-start = (f32[11,8,256]{2,1,0:T(8,128)S(1)}, f32[11,8,256]{2,1,0:T(8,128)S(1)}, u32[]{:S(2)}, u32[]{:S(2)}) collective-permute-start(f32[11,8,256]{2,1,0:T(8,128)S(1)} %get-tuple-element.20), channel_id=1, source_target_pairs={{0,8},{8,16},{16,24},{24,32},{32,40},{40,48},{48,56},{56,64},{64,7... | collective-permute-start | bytes 270344 | tf_op jit(solution)/shard_map/ppermute | solution.py:302
  10.2 6.3 %collective-permute-start.1 = (f32[11,8,256]{2,1,0:T(8,128)S(1)}, f32[11,8,256]{2,1,0:T(8,128)S(1)}, u32[]{:S(2)}, u32[]{:S(2)}) collective-permute-start(f32[11,8,256]{2,1,0:T(8,128)S(1)} %get-tuple-element.21), channel_id=1, source_target_pairs={{0,120},{8,0},{16,8},{24,16},{32,24},{40,32},{48,40},{56,48},{64,5... | collective-permute-start | bytes 270344 | tf_op jit(solution)/shard_map/ppermute | solution.py:302
  16.7 8.2 %collective-permute-start.4 = (f32[11,3,128]{2,1,0:T(4,128)S(1)}, f32[11,3,128]{2,1,0:T(4,128)S(1)}, u32[]{:S(2)}, u32[]{:S(2)}) collective-permute-start(f32[11,3,128]{2,1,0:T(4,128)S(1)} %get-tuple-element.22), channel_id=1, source_target_pairs={{0,1},{1,2},{2,3},{3,4},{4,5},{5,6},{6,7},{7,0},{8,9},{9,10},{10,1... | collective-permute-start | bytes 50696 | tf_op jit(solution)/shard_map/ppermute | solution.py:302
  19.8 5.3 %collective-permute-start.5 = (f32[11,3,128]{2,1,0:T(4,128)S(1)}, f32[11,3,128]{2,1,0:T(4,128)S(1)}, u32[]{:S(2)}, u32[]{:S(2)}) collective-permute-start(f32[11,3,128]{2,1,0:T(4,128)S(1)} %get-tuple-element.23), channel_id=1, source_target_pairs={{0,7},{1,0},{2,1},{3,2},{4,3},{5,4},{6,5},{7,6},{8,15},{9,8},{10,9... | collective-permute-start | bytes 50696 | tf_op jit(solution)/shard_map/ppermute | solution.py:302
